TPU v7x, 32 devices: a whole 2x2x4 slice. The times are simulated.
32 devices in a mesh: nodes: 32 (over z, y, x, core).
Axes of the slice: x: 2, y: 2, z: 4, core: 2. Of those that a mesh axis runs over, the one named last changes fastest.
Arguments:
- features: bfloat16 [32768, 128], P('nodes'), may hold values from 0 to 2
- send_lists: int32 [32, 32, 16], P('nodes'), may hold values from 0 to 1023
- hub_rows: int32 [2048], P('nodes'), may hold values from 0 to 1023
- local_tiles: bfloat16 [3072, 128, 128], P('nodes'), may hold values from 0 to 2, as said below
- local_dst: int32 [3072], P('nodes'), may hold values from 0 to 7
- local_src: int32 [3072], P('nodes'), may hold values from 0 to 7
- remote_tiles: bfloat16 [3072, 128, 128], P('nodes'), may hold values from 0 to 2, as said below
- remote_dst: int32 [3072], P('nodes'), may hold values from 0 to 7
- remote_src: int32 [3072], P('nodes'), may hold values from 0 to 3
- hub_tiles: bfloat16 [3072, 128, 128], P('nodes'), may hold values from 0 to 2, as said below
- hub_dst: int32 [3072], P('nodes'), may hold values from 0 to 7
- hub_src: int32 [3072], P('nodes'), may hold values from 0 to 15
- self_one: bfloat16 [128, 256], replicated, may hold values from -0.5 to 0.5
- neigh_one: bfloat16 [128, 256], replicated, may hold values from -0.5 to 0.5
- self_two: bfloat16 [256, 256], replicated, may hold values from -0.375 to 0.375
- neigh_two: bfloat16 [256, 256], replicated, may hold values from -0.375 to 0.375
Outputs:
- embedding: float32 [32768, 256], P('nodes')
Inputs may be any that keep to these rules, and one draw needn't show every extreme that they name: `local_tiles`: tile entries are zero or positive edge weights; about one entry in 128 is nonzero. `remote_tiles`: tile entries are zero or positive edge weights; about one entry in 128 is nonzero. `hub_tiles`: tile entries are zero or positive edge weights; about one entry in 128 is nonzero.
All inputs are finite; a program needn't handle non-finite values.
Results may differ from a plain program's by a relative error of at most 0.0033.
Values may be sent and summed in bfloat16 or wider, within the bound.
No kernel may reach another device: no remote copies, remote signals or barrier semaphores. Data moves between devices by JAX's collectives and lax.ppermute only.
A program may use at most 128 MiB of HBM per device.

v0:
```python
import jax
import jax.numpy as jnp
from jax import lax
from jax.sharding import PartitionSpec as P


def aggregate(tiles, dst, src, source, blocks_out):
    size = tiles.shape[1]
    width = source.shape[1]
    blocks = source.reshape(-1, size, width)[src]
    prod = jnp.einsum("tij,tjf->tif", tiles, blocks, preferred_element_type=jnp.float32)
    total = jax.ops.segment_sum(prod, dst, num_segments=blocks_out)
    return total.reshape(blocks_out * size, width)


def row_weight(tiles, dst, blocks_out):
    sums = jnp.sum(tiles.astype(jnp.float32), axis=2)
    return jax.ops.segment_sum(sums, dst, num_segments=blocks_out).reshape(-1)


def collect(values, lists, hub_rows):
    width = values.shape[1]
    outgoing = values[lists]
    mine = values[hub_rows]
    arrived = lax.all_to_all(outgoing, "nodes", split_axis=0, concat_axis=0, tiled=True)
    remote = arrived.reshape(-1, width)
    hubs = lax.all_gather(mine, "nodes", axis=0, tiled=True)
    return (remote, hubs)


def layer(values, lists, hub_rows, groups, degree, w_self, w_neigh):
    lt, ld, ls, rt, rd, rs, ht, hd, hs = groups
    blocks_out = values.shape[0] // lt.shape[1]
    remote, hubs = collect(values, lists, hub_rows)
    agg = aggregate(lt, ld, ls, values, blocks_out)
    agg = agg + aggregate(rt, rd, rs, remote, blocks_out)
    agg = agg + aggregate(ht, hd, hs, hubs, blocks_out)
    mean = (agg / degree[:, None]).astype(jnp.bfloat16)
    out = jnp.dot(values, w_self, preferred_element_type=jnp.float32) + jnp.dot(
        mean, w_neigh, preferred_element_type=jnp.float32
    )
    return jax.nn.relu(out)


def per_device(
    features,
    send_lists,
    hub_rows,
    local_tiles,
    local_dst,
    local_src,
    remote_tiles,
    remote_dst,
    remote_src,
    hub_tiles,
    hub_dst,
    hub_src,
    self_one,
    neigh_one,
    self_two,
    neigh_two,
):
    lists = send_lists[0]
    groups = (
        local_tiles,
        local_dst,
        local_src,
        remote_tiles,
        remote_dst,
        remote_src,
        hub_tiles,
        hub_dst,
        hub_src,
    )
    blocks_out = features.shape[0] // local_tiles.shape[1]
    degree = (
        1.0
        + row_weight(local_tiles, local_dst, blocks_out)
        + row_weight(remote_tiles, remote_dst, blocks_out)
        + row_weight(hub_tiles, hub_dst, blocks_out)
    )
    first = layer(features, lists, hub_rows, groups, degree, self_one, neigh_one).astype(
        jnp.bfloat16
    )
    return layer(first, lists, hub_rows, groups, degree, self_two, neigh_two)


def solution(mesh):
    placed = (
        P("nodes", None),
        P("nodes", None, None),
        P("nodes"),
        P("nodes", None, None),
        P("nodes"),
        P("nodes"),
        P("nodes", None, None),
        P("nodes"),
        P("nodes"),
        P("nodes", None, None),
        P("nodes"),
        P("nodes"),
        P(),
        P(),
        P(),
        P(),
    )
    return jax.shard_map(
        per_device, mesh=mesh, in_specs=placed, out_specs=P("nodes", None), check_vma=False
    )
```

profile of v0, /device:TPU:0, one launch (start us, length us, event | category | flops | bytes accessed | tf_op | source)
XLA Modules:
  0.0 326.3 jit_solution(1839686529260726268)
XLA Ops:
  6.5 0.8 compare_select_fusion
  7.4 0.1 copy.25
  7.5 0.1 reshape.86
  7.6 1.9 gather_fusion.1
  9.5 7.3 %all-to-all-start = ((bf16[32,16,128]{2,1,0:T(8,128)(2,1)}), bf16[32,16,128]{2,1,0:T(8,128)(2,1)S(1)}, u32[]{:S(2)}, u32[]{:S(2)}) async-start(bf16[32,16,128]{2,1,0:T(8,128)(2,1)} %bitcast.61), calls=%async_computation | async-start | bytes 262144 | tf_op jit(solution)/shard_map/all_to_all | solution.py:25
  16.8 0.0 all-gather.4.cloned.1.call-start
  16.8 0.7 compare_select_fusion.3
  17.5 0.7 compare_select_fusion.4
  18.2 3.4 %convert_reduce_fusion.2 = f32[96,128]{1,0:T(8,128)} fusion(bf16[96,128,128]{2,1,0:T(8,128)(2,1)} %param.19), kind=kLoop, calls=%fused_computation.21 | loop fusion | flops 3133440 | bytes 3194880 | tf_op jit(solution)/shard_map/reduce_sum | solution.py:17
  21.6 2.7 gather_fusion
  24.3 0.0 copy-done.2
  24.3 6.9 %convolution_bitcast_fusion.5 = f32[96,128,128]{1,2,0:T(8,128)} fusion(bf16[96,128,128]{2,1,0:T(8,128)(2,1)} %gather_fusion, bf16[96,128,128]{2,1,0:T(8,128)(2,1)S(1)} %copy-done.2), kind=kOutput, calls=%fused_computation.27 | convolution fusion | flops 402653184 | bytes 12582912 | tf_op jit(solution)/shard_map/tij,tjf->tif/dot_general | solution.py:11
  31.2 6.7 %copy.24 = f32[96,128,128]{2,1,0:T(8,128)} copy(f32[96,128,128]{1,2,0:T(8,128)} %convolution_bitcast_fusion.5) | data formatting | bytes 12582912 | tf_op jit(solution)/shard_map/tij,tjf->tif/dot_general | solution.py:11
  38.0 1.2 gather_fusion.3
  39.2 46.2 %all-gather = bf16[2048,128]{1,0:T(8,128)(2,1)} all-gather(bf16[64,128]{1,0:T(8,128)(2,1)} %gather_fusion.3), channel_id=2, replica_groups=mesh['nodes'=32] {'nodes'}, dimensions={0}, use_global_device_ids=true | all-gather | bytes 540672 | tf_op jit(solution)/shard_map/all_gather | solution.py:27
  85.4 0.7 compare_select_fusion.1
  86.0 1.5 convert_reduce_fusion
  87.5 3.8 %gather_fusion.4 = bf16[96,128,128]{2,1,0:T(8,128)(2,1)} fusion(bf16[16,128,128]{2,1,0:T(8,128)(2,1)} %bitcast.60, s32[1024]{0:T(1024)S(1)} %pad_clamp_fusion), kind=kCustom, calls=%fused_computation.4 | custom fusion | bytes 6291840 | tf_op jit(solution)/shard_map/gather | solution.py:10
  91.3 6.8 %convolution_bitcast_fusion.3 = f32[96,128,128]{1,2,0:T(8,128)} fusion(bf16[96,128,128]{2,1,0:T(8,128)(2,1)} %gather_fusion.4, bf16[96,128,128]{2,1,0:T(8,128)(2,1)S(1)} %copy-done.4), kind=kOutput, calls=%fused_computation.25 | convolution fusion | flops 402653184 | bytes 12582912 | tf_op jit(solution)/shard_map/tij,tjf->tif/dot_general | solution.py:11
  98.2 6.7 %copy.29 = f32[96,128,128]{2,1,0:T(8,128)} copy(f32[96,128,128]{1,2,0:T(8,128)} %convolution_bitcast_fusion.3) | data formatting | bytes 12582912 | tf_op jit(solution)/shard_map/tij,tjf->tif/dot_general | solution.py:11
  104.8 1.5 convert_reduce_fusion.1
  106.4 0.0 copy-start.14
  106.4 0.0 copy-start.12
  106.4 0.0 copy-start.9
  106.4 13.2 %scatter_fusion = f32[8,128,128]{2,1,0:T(8,128)S(1)} fusion(f32[8,128,128]{2,1,0:T(8,128)S(1)} %broadcast.58.clone, s32[96]{0:T(128)} %param.20, f32[96,128,128]{2,1,0:T(8,128)} %copy.24), kind=kCustom, calls=%fused_computation.10 | custom fusion | flops 1572864 | bytes 18874752 | tf_op jit(solution)/shard_map/scatter-add | solution.py:12
  119.6 1.3 scatter_custom_fusion.3
  121.0 1.3 scatter_custom_fusion.4
  122.3 1.2 scatter_fusion.3
  123.6 0.3 fusion.9
  123.8 0.0 all-to-all-done
  123.8 2.7 gather_fusion.2
  126.6 7.8 %convolution_bitcast_fusion.4 = f32[96,128,128]{1,2,0:T(8,128)} fusion(bf16[96,128,128]{2,1,0:T(8,128)(2,1)} %gather_fusion.2, bf16[96,128,128]{2,1,0:T(8,128)(2,1)} %param.22), kind=kOutput, calls=%fused_computation.26 | convolution fusion | flops 402653184 | bytes 12582912 | tf_op jit(solution)/shard_map/tij,tjf->tif/dot_general | solution.py:11
  134.4 6.6 %copy.27 = f32[96,128,128]{2,1,0:T(8,128)} copy(f32[96,128,128]{1,2,0:T(8,128)} %convolution_bitcast_fusion.4) | data formatting | bytes 12582912 | tf_op jit(solution)/shard_map/tij,tjf->tif/dot_general | solution.py:11
  141.0 12.9 %scatter_fusion.1 = f32[8,128,128]{2,1,0:T(8,128)S(1)} fusion(f32[8,128,128]{2,1,0:T(8,128)S(1)} %broadcast.58.clone.1, s32[96]{0:T(128)S(1)} %copy-done.14, f32[96,128,128]{2,1,0:T(8,128)} %copy.27), kind=kCustom, calls=%fused_computation.11 | custom fusion | flops 1572864 | bytes 18874752 | tf_op jit(solution)/shard_map/scatter-add | solution.py:12
  153.9 0.1 add.98
  154.0 0.0 copy-start.10
  154.0 12.9 %scatter_fusion.2 = f32[8,128,128]{2,1,0:T(8,128)S(1)} fusion(f32[8,128,128]{2,1,0:T(8,128)S(1)} %add.98, s32[96]{0:T(128)S(1)} %copy-done.12, f32[96,128,128]{2,1,0:T(8,128)} %copy.29), kind=kCustom, calls=%fused_computation.12 | custom fusion | flops 1572864 | bytes 18874752 | tf_op jit(solution)/shard_map/scatter-add | solution.py:12
  166.9 0.2 fusion.4
  167.2 0.3 fusion.2
  167.4 1.4 gather_fusion.8
  168.9 0.0 all-gather.4.cloned.1.call-update
  168.9 2.6 gather_fusion.6
  171.5 2.6 all-to-all-start.1
  174.1 5.9 %gather_fusion.5 = bf16[96,128,256]{2,1,0:T(8,128)(2,1)} fusion(bf16[8,128,256]{2,1,0:T(8,128)(2,1)S(1)} %bitcast.54, s32[1024]{0:T(1024)S(1)} %pad_clamp_fusion.4), kind=kCustom, calls=%fused_computation.5 | custom fusion | bytes 12583296 | tf_op jit(solution)/shard_map/gather | solution.py:10
  180.0 10.1 %convolution_bitcast_fusion.2 = f32[96,128,256]{1,2,0:T(8,128)} fusion(bf16[96,128,256]{2,1,0:T(8,128)(2,1)} %gather_fusion.5, bf16[96,128,128]{2,1,0:T(8,128)(2,1)} %param.19), kind=kOutput, calls=%fused_computation.24 | convolution fusion | flops 805306368 | bytes 22020096 | tf_op jit(solution)/shard_map/tij,tjf->tif/dot_general | solution.py:11
  190.1 12.6 %copy.31 = f32[96,128,256]{2,1,0:T(8,128)} copy(f32[96,128,256]{1,2,0:T(8,128)} %convolution_bitcast_fusion.2) | data formatting | bytes 25165824 | tf_op jit(solution)/shard_map/tij,tjf->tif/dot_general | solution.py:11
  202.7 0.1 broadcast.69.clone
  202.8 0.0 copy-start.7
  202.8 18.3 %scatter_fusion.4 = f32[8,128,256]{2,1,0:T(8,128)S(1)} fusion(f32[8,128,256]{2,1,0:T(8,128)S(1)} %broadcast.69.clone, s32[96]{0:T(128)S(1)} %copy-done.13, f32[96,128,256]{2,1,0:T(8,128)} %copy.31), kind=kCustom, calls=%fused_computation.16 | custom fusion | flops 3145728 | bytes 37749120 | tf_op jit(solution)/shard_map/scatter-add | solution.py:12
  221.2 1.3 fusion.10
  222.4 0.0 all-to-all-done.1
  222.4 5.9 %gather_fusion.7 = bf16[96,128,256]{2,1,0:T(8,128)(2,1)} fusion(bf16[4,128,256]{2,1,0:T(8,128)(2,1)S(1)} %bitcast.55, s32[1024]{0:T(1024)S(1)} %pad_clamp_fusion.2), kind=kCustom, calls=%fused_computation.7 | custom fusion | bytes 12583296 | tf_op jit(solution)/shard_map/gather | solution.py:10
  228.3 10.1 %convolution_bitcast_fusion.1 = f32[96,128,256]{1,2,0:T(8,128)} fusion(bf16[96,128,256]{2,1,0:T(8,128)(2,1)} %gather_fusion.7, bf16[96,128,128]{2,1,0:T(8,128)(2,1)} %param.22), kind=kOutput, calls=%fused_computation.23 | convolution fusion | flops 805306368 | bytes 22020096 | tf_op jit(solution)/shard_map/tij,tjf->tif/dot_general | solution.py:11
  238.5 12.6 %copy.33 = f32[96,128,256]{2,1,0:T(8,128)} copy(f32[96,128,256]{1,2,0:T(8,128)} %convolution_bitcast_fusion.1) | data formatting | bytes 25165824 | tf_op jit(solution)/shard_map/tij,tjf->tif/dot_general | solution.py:11
  251.1 0.1 broadcast.69.clone.1
  251.2 18.3 %scatter_fusion.5 = f32[8,128,256]{2,1,0:T(8,128)S(1)} fusion(f32[8,128,256]{2,1,0:T(8,128)S(1)} %broadcast.69.clone.1, s32[96]{0:T(128)S(1)} %copy-done.15, f32[96,128,256]{2,1,0:T(8,128)} %copy.33), kind=kCustom, calls=%fused_computation.17 | custom fusion | flops 3145728 | bytes 37749120 | tf_op jit(solution)/shard_map/scatter-add | solution.py:12
  269.4 0.1 add.105
  269.6 0.0 all-gather.4.cloned.1.call-done
  269.6 7.4 %gather_fusion.9 = bf16[96,128,256]{2,1,0:T(8,128)(2,1)} fusion(bf16[16,128,256]{2,1,0:T(8,128)(2,1)} %bitcast.59, s32[1024]{0:T(1024)S(1)} %pad_clamp_fusion), kind=kCustom, calls=%fused_computation.9 | custom fusion | bytes 12583296 | tf_op jit(solution)/shard_map/gather | solution.py:10
  277.0 10.1 %convolution_bitcast_fusion = f32[96,128,256]{1,2,0:T(8,128)} fusion(bf16[96,128,256]{2,1,0:T(8,128)(2,1)} %gather_fusion.9, bf16[96,128,128]{2,1,0:T(8,128)(2,1)} %param.25), kind=kOutput, calls=%fused_computation.22 | convolution fusion | flops 805306368 | bytes 22020096 | tf_op jit(solution)/shard_map/tij,tjf->tif/dot_general | solution.py:11
  287.1 12.6 %copy.35 = f32[96,128,256]{2,1,0:T(8,128)} copy(f32[96,128,256]{1,2,0:T(8,128)} %convolution_bitcast_fusion) | data formatting | bytes 25165824 | tf_op jit(solution)/shard_map/tij,tjf->tif/dot_general | solution.py:11
  299.7 18.3 %scatter_fusion.6 = f32[8,128,256]{2,1,0:T(8,128)S(1)} fusion(f32[8,128,256]{2,1,0:T(8,128)S(1)} %add.105, s32[96]{0:T(128)S(1)} %copy-done.12, f32[96,128,256]{2,1,0:T(8,128)} %copy.35), kind=kCustom, calls=%fused_computation.18 | custom fusion | flops 3145728 | bytes 37749120 | tf_op jit(solution)/shard_map/scatter-add | solution.py:12
  318.0 0.2 fusion.3
  318.2 1.3 fusion
  (37 shorter events, 0.2 us)
Async XLA Ops:
  6.5 1.0 copy-start
  6.5 17.8 %copy-start.2 = (bf16[96,128,128]{2,1,0:T(8,128)(2,1)S(1)}, bf16[96,128,128]{2,1,0:T(8,128)(2,1)}, u32[]{:S(2)}) copy-start(bf16[96,128,128]{2,1,0:T(8,128)(2,1)} %param.19) | copy-start | bytes 9437188
  9.5 114.4 %all-to-all-start = ((bf16[32,16,128]{2,1,0:T(8,128)(2,1)}), bf16[32,16,128]{2,1,0:T(8,128)(2,1)S(1)}, u32[]{:S(2)}, u32[]{:S(2)}) async-start(bf16[32,16,128]{2,1,0:T(8,128)(2,1)} %bitcast.61), calls=%async_computation | async-start | bytes 262144 | tf_op jit(solution)/shard_map/all_to_all | solution.py:25
  16.8 252.8 %all-gather.4.cloned.1.call-start = ((), (), s32[]{:S(2)}) async-start(), calls=%async_computation.2 | async-start | bytes 1081344 | tf_op jit(solution)/shard_map/all_gather | solution.py:27
  31.2 6.8 %copy-start.16 = (s32[64]{0:T(128)S(1)}, s32[64]{0:T(128)}, u32[]{:S(2)}) copy-start(s32[64]{0:T(128)} %param.18) | copy-start | bytes 772
  31.2 54.8 %copy-start.4 = (bf16[96,128,128]{2,1,0:T(8,128)(2,1)S(1)}, bf16[96,128,128]{2,1,0:T(8,128)(2,1)}, u32[]{:S(2)}) copy-start(bf16[96,128,128]{2,1,0:T(8,128)(2,1)} %param.25) | copy-start | bytes 9437188
  38.0 47.4 %copy-start.11 = (s32[1024]{0:T(1024)}, s32[1024]{0:T(1024)S(1)}, u32[]{:S(2)}) copy-start(s32[1024]{0:T(1024)S(1)} %pad_clamp_fusion.1) | copy-start | bytes 12292
  98.2 6.7 %copy-start.3 = (bf16[96,128,128]{2,1,0:T(8,128)(2,1)S(1)}, bf16[96,128,128]{2,1,0:T(8,128)(2,1)}, u32[]{:S(2)}) copy-start(bf16[96,128,128]{2,1,0:T(8,128)(2,1)} %param.22) | copy-start | bytes 9437188
  106.4 14.5 %copy-start.14 = (s32[96]{0:T(128)S(1)}, s32[96]{0:T(128)}, u32[]{:S(2)}) copy-start(s32[96]{0:T(128)} %param.23) | copy-start | bytes 1156
  106.4 15.9 %copy-start.6 = (f32[96,128]{1,0:T(8,128)S(1)}, f32[96,128]{1,0:T(8,128)}, u32[]{:S(2)}) copy-start(f32[96,128]{1,0:T(8,128)} %convert_reduce_fusion) | copy-start | bytes 147460
  106.4 15.9 %copy-start.12 = (s32[96]{0:T(128)S(1)}, s32[96]{0:T(128)}, u32[]{:S(2)}) copy-start(s32[96]{0:T(128)} %param.26) | copy-start | bytes 1156
  106.4 17.1 %copy-start.9 = (bf16[128,256]{1,0:T(8,128)(2,1)S(1)}, bf16[128,256]{1,0:T(8,128)(2,1)}, u32[]{:S(2)}) copy-start(bf16[128,256]{1,0:T(8,128)(2,1)} %param.28) | copy-start | bytes 196612
  154.0 13.1 %copy-start.10 = (bf16[128,256]{1,0:T(8,128)(2,1)S(1)}, bf16[128,256]{1,0:T(8,128)(2,1)}, u32[]{:S(2)}) copy-start(bf16[128,256]{1,0:T(8,128)(2,1)} %param.29) | copy-start | bytes 196612
  171.5 51.0 %all-to-all-start.1 = ((bf16[32,16,256]{2,1,0:T(8,128)(2,1)}), bf16[32,16,256]{2,1,0:T(8,128)(2,1)S(1)}, u32[]{:S(2)}, u32[]{:S(2)}) async-start(bf16[32,16,256]{2,1,0:T(8,128)(2,1)} %bitcast.12), calls=%async_computation.1 | async-start | bytes 524288 | tf_op jit(solution)/shard_map/all_to_all | solution.py:25
  190.1 12.7 %copy-start.13 = (s32[96]{0:T(128)S(1)}, s32[96]{0:T(128)}, u32[]{:S(2)}) copy-start(s32[96]{0:T(128)} %param.20) | copy-start | bytes 1156
  202.8 18.3 %copy-start.7 = (bf16[256,256]{1,0:T(8,128)(2,1)S(1)}, bf16[256,256]{1,0:T(8,128)(2,1)}, u32[]{:S(2)}) copy-start(bf16[256,256]{1,0:T(8,128)(2,1)} %param.30) | copy-start | bytes 393220
  238.5 12.7 %copy-start.15 = (s32[96]{0:T(128)S(1)}, s32[96]{0:T(128)}, u32[]{:S(2)}) copy-start(s32[96]{0:T(128)} %param.23) | copy-start | bytes 1156
  299.7 18.5 %copy-start.5 = (f32[1024,256]{1,0:T(8,128)S(1)}, f32[1024,256]{1,0:T(8,128)}, u32[]{:S(2)}) copy-start(f32[1024,256]{1,0:T(8,128)} %fusion.10) | copy-start | bytes 3145732
  299.7 18.5 %copy-start.8 = (bf16[256,256]{1,0:T(8,128)(2,1)S(1)}, bf16[256,256]{1,0:T(8,128)(2,1)}, u32[]{:S(2)}) copy-start(bf16[256,256]{1,0:T(8,128)(2,1)} %param.31) | copy-start | bytes 393220
  299.7 19.8 %copy-start.1 = (bf16[1024,128]{1,0:T(8,128)(2,1)S(1)}, bf16[1024,128]{1,0:T(8,128)(2,1)}, u32[]{:S(2)}) copy-start(bf16[1024,128]{1,0:T(8,128)(2,1)} %param.16) | copy-start | bytes 786436
Sparse Core Ops, SparseCore 0:
  169.0 50.5 all-gather.3
where the time goes:
time: 329 us; the launch traced here: 326 us
  other arithmetic  108 us (33%)
  local copies, waits for them, and re-layouts  93.8 us (29%)
  matrix products  55 us (17%)
  blocking collectives  46.2 us (14%)
  between operations  13.7 us (4%)
  starting transfers between devices  9.92 us (3%)
    scatter-add x6, other arithmetic, aggregate(): total = jax.ops.segment_sum(prod, dst, num_segments=blocks_out)  93.8 us
    dot_general x6, local copies, waits for them, and re-layouts, aggregate(): jnp.einsum('tij,tjf->tif', tiles, blocks, preferred_element_type=jnp.floa...  57.8 us
    dot_general x6, matrix products, aggregate(): jnp.einsum('tij,tjf->tif', tiles, blocks, preferred_element_type=jnp.floa...  51.9 us
    all_gather x1, blocking collectives, collect(): hubs = lax.all_gather(mine, 'nodes', axis=0, tiled=True)  46.2 us
    gather x6, local copies, waits for them, and re-layouts, aggregate(): blocks = source.reshape(-1, size, width)[src]  28.4 us
    all_to_all x2, starting transfers between devices, collect(): lax.all_to_all(outgoing, 'nodes', split_axis=0, concat_axis=0, tiled=True)  9.88 us
  transfers between devices with their start and end apart: 3, of which 0 were waited for; matrix products, arithmetic and copies ran while one was open for 49% of the time, Pallas kernels for 0%

commit v1 on v0

v1 whole, which is shorter than its diff:
```python
import functools

import jax
import jax.numpy as jnp
from jax import lax
from jax.experimental import pallas as pl
from jax.experimental.pallas import tpu as pltpu
from jax.sharding import PartitionSpec as P

F32 = jnp.float32
BF16 = jnp.bfloat16
MIB = 1024 * 1024


def params(mib):
    return pltpu.CompilerParams(vmem_limit_bytes=mib * MIB)


def whole(memory=pltpu.VMEM):
    return pl.BlockSpec(memory_space=memory)


def dot(a, b):
    return jnp.dot(a, b, preferred_element_type=F32)


def column(row, first, rows):
    shape = (rows, row.shape[1])
    sub = lax.broadcasted_iota(jnp.int32, shape, 0)
    lane = lax.broadcasted_iota(jnp.int32, shape, 1)
    picked = jnp.where(lane == sub + first, jnp.broadcast_to(row, shape), 0.0)
    return jnp.sum(picked, axis=1, keepdims=True)


def fill_send(send_rows, sel_ref, values, send_ref):
    peers = send_ref.shape[0]
    hubs = sel_ref.shape[0] - peers * send_rows
    half = hubs // 2
    rows = dot(sel_ref[...], values).astype(BF16)
    for p in range(peers):
        send_ref[p, 0:send_rows, :] = rows[p * send_rows : (p + 1) * send_rows]
        start = peers * send_rows + half * (p % 2)
        send_ref[p, send_rows : send_rows + half, :] = rows[start : start + half]


def select_kernel(x_ref, lists_ref, hub_ref, sel_ref, send_ref):
    peers, send_rows = lists_ref.shape[1:]
    nodes = x_ref.shape[0]
    hubs = hub_ref.shape[1]
    place = lax.broadcasted_iota(jnp.int32, (16, nodes), 1).astype(F32)

    def put(start, col):
        sel_ref[start : start + 16, :] = jnp.where(col == place, 1.0, 0.0).astype(BF16)

    for p in range(peers):
        row = lists_ref[0, p : p + 1, :].astype(F32)
        for c in range(0, send_rows, 16):
            put(p * send_rows + c, column(row, c, 16))
    hub_row = hub_ref[...].astype(F32)
    for c in range(0, hubs, 16):
        put(peers * send_rows + c, column(hub_row, c, 16))
    fill_send(send_rows, sel_ref, x_ref[...], send_ref)


def build_kernel(
    cols, parts, steps, ld, ls, rd, rs, hd, hs, x_ref, lt, rt, ht, al_ref, ar_ref, inv_ref, agg_ref, acc
):
    part = pl.program_id(0)
    step = pl.program_id(1)
    size = acc.shape[1]
    blocks = acc.shape[0] // sum(cols)
    wide = sum(cols)
    per = lt.shape[0]

    @pl.when(step == 0)
    def _():
        def clear(i, _):
            acc[i] = jnp.zeros((size, size), F32)
            return 0

        lax.fori_loop(0, blocks * wide, clear, 0)

    def add(i, _):
        t = step * per + i
        off = 0
        for dst, src, tiles, width in ((ld, ls, lt, cols[0]), (rd, rs, rt, cols[1]), (hd, hs, ht, cols[2])):
            d = dst[t]
            slot = d * wide + off + src[t]
            if parts > 1:
                low = part * blocks
                inside = jnp.logical_and(d >= low, d < low + blocks)
                slot = jnp.where(inside, slot - low * wide, blocks * wide)
            acc[slot] += tiles[i].astype(F32)
            off += width
        return 0

    lax.fori_loop(0, per, add, 0)

    @pl.when(step == steps - 1)
    def _():
        def finish(b, _):
            rows = pl.ds(pl.multiple_of(b * size, size), size)
            total = jnp.zeros((size, size), F32)
            for c in range(wide):
                tile = acc[b * wide + c]
                total += tile
                ref, at = (al_ref, c) if c < cols[0] else (ar_ref, c - cols[0])
                ref[rows, at * size : (at + 1) * size] = tile.astype(BF16)
            deg = 1.0 + jnp.sum(total, axis=1, keepdims=True)
            inv_ref[rows, :] = jnp.broadcast_to(1.0 / deg, (size, size))
            agg_ref[rows, :] = dot(al_ref[rows, :], x_ref[...])
            return 0

        lax.fori_loop(0, blocks, finish, 0)


def assemble(send_rows, own_ref, other_ref, dest_ref, lanes):
    peers, per = own_ref.shape[:2]
    half = per - send_rows
    mine = lax.rem(lax.axis_index("nodes"), 2)
    base = peers * send_rows
    for o in range(peers):
        dest_ref[o * send_rows : (o + 1) * send_rows, lanes] = own_ref[o, 0:send_rows, :]
        for ref, h in ((own_ref, mine), (other_ref, 1 - mine)):
            at = pl.multiple_of(base + o * 2 * half + h * half, half)
            dest_ref[pl.ds(at, half), lanes] = ref[o, send_rows:per, :]


def mean_kernel(
    send_rows, parts, own_ref, other_ref, ar_ref, agg_ref, inv_ref, sel_ref, mean_ref, send_ref, xr_ref
):
    part = pl.program_id(0)
    rows = ar_ref.shape[0]

    @pl.when(part == 0)
    def _():
        assemble(send_rows, own_ref, other_ref, xr_ref, slice(None))

    agg = agg_ref[...] + dot(ar_ref[...], xr_ref[...])
    mean_ref[pl.ds(pl.multiple_of(part * rows, rows), rows), :] = (agg * inv_ref[...]).astype(BF16)

    @pl.when(part == parts - 1)
    def _():
        fill_send(send_rows, sel_ref, mean_ref[...], send_ref)


def own_kernel(x_ref, mean_ref, al_ref, self_one, neigh_one, self_two, agg_ref, part_ref, first):
    part = pl.program_id(0)

    @pl.when(part == 0)
    def _():
        total = dot(x_ref[...], self_one[...]) + dot(mean_ref[...], neigh_one[...])
        first[...] = jnp.maximum(total, 0.0).astype(BF16)

    rows = al_ref.shape[0]
    agg_ref[...] = dot(al_ref[...], first[...])
    at = pl.ds(pl.multiple_of(part * rows, rows), rows)
    part_ref[...] = dot(first[at, :], self_two[...])


def last_kernel(
    send_rows,
    own_ref,
    other_ref,
    xr_ref,
    self_one,
    neigh_one,
    ar_ref,
    agg_ref,
    part_ref,
    inv_ref,
    neigh_two,
    out_ref,
    both,
    weight,
    first,
):
    width = xr_ref.shape[1]

    @pl.when(pl.program_id(0) == 0)
    def _():
        both[:, 0:width] = xr_ref[...]
        assemble(send_rows, own_ref, other_ref, both, slice(width, 2 * width))
        weight[0:width, :] = self_one[...]
        weight[width : 2 * width, :] = neigh_one[...]
        first[...] = jnp.maximum(dot(both[...], weight[...]), 0.0).astype(BF16)

    agg = agg_ref[...] + dot(ar_ref[...], first[...])
    inv = inv_ref[...]
    inv = jnp.concatenate([inv] * (agg.shape[1] // inv.shape[1]), axis=1)
    mean = (agg * inv).astype(BF16)
    out_ref[...] = jnp.maximum(part_ref[...] + dot(mean, neigh_two[...]), 0.0)


def per_device(
    features,
    send_lists,
    hub_rows,
    local_tiles,
    local_dst,
    local_src,
    remote_tiles,
    remote_dst,
    remote_src,
    hub_tiles,
    hub_dst,
    hub_src,
    self_one,
    neigh_one,
    self_two,
    neigh_two,
):
    nodes, f_in = features.shape
    hid = self_one.shape[1]
    tiles, size = local_tiles.shape[:2]
    _, peers, send_rows = send_lists.shape
    hubs = hub_rows.shape[0]
    per = send_rows + hubs // 2
    far = peers * (send_rows + hubs)
    cols = (nodes // size, peers * send_rows // size, peers * hubs // size)
    wide = sum(cols)
    blocks = nodes // size
    parts = 1
    while blocks * wide * size * size * 4 > parts * 16 * MIB:
        parts *= 2
    rows = nodes // parts
    spare = 0 if parts == 1 else 1
    swap = [(i, i ^ 1) for i in range(peers)]
    sds = jax.ShapeDtypeStruct
    vm = whole()

    def split(width):
        return vm if parts == 1 else pl.BlockSpec((rows, width), lambda i, *_: (i, 0))

    sel, send = pl.pallas_call(
        select_kernel,
        out_shape=(sds((peers * send_rows + hubs, nodes), BF16), sds((peers, per, f_in), BF16)),
        in_specs=[vm] * 3,
        out_specs=(vm, vm),
        compiler_params=params(32),
        name="select",
    )(features, send_lists, hub_rows.reshape(1, hubs))

    got = lax.all_to_all(send, "nodes", split_axis=0, concat_axis=0, tiled=True)

    steps = 6
    chunk = pl.BlockSpec((tiles // steps, size, size), lambda i, j, *_: (j, 0, 0))
    one = pl.Buffered(1)

    def block_out(width):
        return pl.BlockSpec((rows, width), lambda i, j, *_: (i, 0), pipeline_mode=one if parts == 1 else None)

    a_local, a_far, inv, agg = pl.pallas_call(
        functools.partial(build_kernel, cols, parts, steps),
        out_shape=(
            sds((nodes, nodes), BF16),
            sds((nodes, far), BF16),
            sds((nodes, size), F32),
            sds((nodes, f_in), F32),
        ),
        grid_spec=pltpu.PrefetchScalarGridSpec(
            num_scalar_prefetch=6,
            grid=(parts, steps),
            in_specs=[vm, chunk, chunk, chunk],
            out_specs=(block_out(nodes), block_out(far), block_out(size), block_out(f_in)),
            scratch_shapes=[pltpu.VMEM((blocks // parts * wide + spare, size, size), F32)],
        ),
        compiler_params=params(48),
        cost_estimate=pl.CostEstimate(flops=2 * nodes * nodes * f_in, bytes_accessed=40 * MIB, transcendentals=0),
        name="build",
    )(
        local_dst,
        local_src,
        remote_dst,
        remote_src,
        hub_dst,
        hub_src,
        features,
        local_tiles,
        remote_tiles,
        hub_tiles,
    )

    other = lax.ppermute(got, "nodes", swap)

    mean, send, x_far = pl.pallas_call(
        functools.partial(mean_kernel, send_rows, parts),
        out_shape=(sds((nodes, f_in), BF16), sds(send.shape, BF16), sds((far, f_in), BF16)),
        grid=(parts,),
        in_specs=[vm, vm, split(far), split(f_in), split(size), vm],
        out_specs=(vm, vm, vm),
        compiler_params=params(40),
        name="mean",
    )(got, other, a_far, agg, inv, sel)

    got = lax.all_to_all(send, "nodes", split_axis=0, concat_axis=0, tiled=True)

    agg, part = pl.pallas_call(
        own_kernel,
        out_shape=(sds((nodes, hid), F32), sds((nodes, hid), F32)),
        grid=(parts,),
        in_specs=[vm, vm, split(nodes), vm, vm, vm],
        out_specs=(split(hid), split(hid)),
        scratch_shapes=[pltpu.VMEM((nodes, hid), BF16)],
        compiler_params=params(32),
        cost_estimate=pl.CostEstimate(flops=2 * nodes * nodes * hid, bytes_accessed=20 * MIB, transcendentals=0),
        name="own",
    )(features, mean, a_local, self_one, neigh_one, self_two)

    other = lax.ppermute(got, "nodes", swap)

    return pl.pallas_call(
        functools.partial(last_kernel, send_rows),
        out_shape=sds((nodes, hid), F32),
        grid=(parts,),
        in_specs=[vm, vm, vm, vm, vm, split(far), split(hid), split(hid), split(size), vm],
        out_specs=split(hid),
        scratch_shapes=[
            pltpu.VMEM((far, 2 * f_in), BF16),
            pltpu.VMEM((2 * f_in, hid), BF16),
            pltpu.VMEM((far, hid), BF16),
        ],
        compiler_params=params(48),
        name="last",
    )(got, other, x_far, self_one, neigh_one, a_far, agg, part, inv, neigh_two)


def solution(mesh):
    placed = (
        P("nodes", None),
        P("nodes", None, None),
        P("nodes"),
        P("nodes", None, None),
        P("nodes"),
        P("nodes"),
        P("nodes", None, None),
        P("nodes"),
        P("nodes"),
        P("nodes", None, None),
        P("nodes"),
        P("nodes"),
        P(),
        P(),
        P(),
        P(),
    )
    return jax.shard_map(
        per_device, mesh=mesh, in_specs=placed, out_specs=P("nodes", None), check_vma=False
    )
```

time: 329 us -> 69.8 us (0.21)
  other arithmetic: 108 us -> 0 us
  local copies, waits for them, and re-layouts: 93.8 us -> 9.76 us
  matrix products: 55 us -> 0 us
  Pallas kernels: 0 us -> 23.3 us
  between operations: 13.7 us -> 0.07 us
  blocking collectives: 46.2 us -> 36 us
  starting transfers between devices: 9.92 us -> 0.01 us
    scatter-add x9 -> x0, other arithmetic: 97.7 us -> none  [the longest x6 93.8 us: aggregate(): total = jax.ops.segment_sum(prod, dst, num_segments=blocks_out)]
    dot_general x6 -> x0, local copies, waits for them, and re-layouts: 57.8 us -> none  [aggregate(): jnp.einsum('tij,tjf->tif', tiles, blocks, preferred_element_type=jnp.floa...]
    dot_general x10 -> x0, matrix products: 55 us -> none  [the longest x6 51.9 us: aggregate(): jnp.einsum('tij,tjf->tif', tiles, blocks, preferred_element_type=jnp.floa...]
    all_gather x1 -> x0, blocking collectives: 46.2 us -> none  [collect(): hubs = lax.all_gather(mine, 'nodes', axis=0, tiled=True)]
    all_to_all x0 -> x2, blocking collectives: none -> 36 us  [per_device(): got = lax.all_to_all(send, 'nodes', split_axis=0, concat_axis=0, tiled=True)]
    gather x10 -> x0, local copies, waits for them, and re-layouts: 35.6 us -> none  [the longest x6 28.4 us: aggregate(): blocks = source.reshape(-1, size, width)[src]]
    pallas_call x0 -> x5, Pallas kernels: none -> 23.3 us  [the longest x1 12.6 us: per_device(): pl.pallas_call(functools.partial(build_kernel, cols, parts, steps), out_s...]
    all_to_all x2 -> x0, starting transfers between devices: 9.88 us -> none  [collect(): lax.all_to_all(outgoing, 'nodes', split_axis=0, concat_axis=0, tiled=True)]
  transfers between devices with their start and end apart: 3 -> 2, of which waited for: 0 -> 1; matrix products, arithmetic and copies ran while one was open for 49% -> 0% of each run, Pallas kernels for 0% -> 20%
where the time goes in v1:
time: 69.8 us; the launch traced here: 69.3 us
  blocking collectives  36 us (52%)
  Pallas kernels  23.3 us (33%)
  local copies, waits for them, and re-layouts  9.76 us (14%)
    all_to_all x2, blocking collectives, per_device(): got = lax.all_to_all(send, 'nodes', split_axis=0, concat_axis=0, tiled=True)  36 us
    pallas_call x1, Pallas kernels, per_device(): pl.pallas_call(functools.partial(build_kernel, cols, parts, steps), out_s...  12.6 us
    unnamed x31, local copies, waits for them, and re-layouts  9.76 us
    pallas_call x1, Pallas kernels, per_device(): pl.pallas_call(functools.partial(last_kernel, send_rows), out_shape=sds((...  6 us
    pallas_call x1, Pallas kernels, per_device(): pl.pallas_call(functools.partial(mean_kernel, send_rows, parts), out_shap...  2.52 us
    pallas_call x1, Pallas kernels, per_device(): pl.pallas_call(own_kernel, out_shape=(sds((nodes, hid), F32), sds((nodes,...  1.53 us
  transfers between devices with their start and end apart: 2, of which 1 were waited for; matrix products, arithmetic and copies ran while one was open for 0% of the time, Pallas kernels for 20%

profile of v1, /device:TPU:0, one launch (start us, length us, event | category | flops | bytes accessed | tf_op | source)
XLA Modules:
  0.0 69.3 jit_solution(2094308304881110909)
XLA Ops:
  0.0 0.8 %copy.17.lists_ref = s32[1,32,16]{2,1,0:T(8,128)S(1)} copy(s32[1,32,16]{1,2,0:T(8,128)} %param.17) | data formatting | bytes 4096 | tf_op args[1]
  0.8 0.0 copy-start.1
  0.8 0.9 %copy-done.1 = bf16[1024,128]{1,0:T(8,128)(2,1)S(1)} copy-done((bf16[1024,128]{1,0:T(8,128)(2,1)S(1)}, bf16[1024,128]{1,0:T(8,128)(2,1)}, u32[]{:S(2)}) %copy-start.1) | copy-done | bytes 262168
  1.7 0.0 copy-start.8
  1.7 0.7 copy-done.8
  2.4 0.6 select.1
  3.0 20.3 %all_to_all.10.own_ref = bf16[32,48,128]{2,1,0:T(8,128)(2,1)S(1)} all-to-all(bf16[32,48,128]{2,1,0:T(8,128)(2,1)S(1)} %get-tuple-element.16), channel_id=1, replica_groups=mesh['nodes'=32] {'nodes'}, dimensions={0} | all-to-all | bytes 786432 | tf_op jit(solution)/shard_map/all_to_all | solution.py:244
  23.3 0.0 collective-permute-start
  23.3 0.0 copy-start.2
  23.3 0.9 %copy-done.2 = bf16[1024,128]{1,0:T(8,128)(2,1)S(1)} copy-done((bf16[1024,128]{1,0:T(8,128)(2,1)S(1)}, bf16[1024,128]{1,0:T(8,128)(2,1)}, u32[]{:S(2)}) %copy-start.2) | copy-done | bytes 262168
  24.2 0.0 copy-start.9
  24.2 0.7 copy-done.9
  24.9 0.0 copy-start.10
  24.9 0.7 copy-done.10
  25.5 0.0 copy-start.11
  25.5 0.7 copy-done.11
  26.2 0.0 copy-start.12
  26.2 0.7 copy-done.12
  26.8 0.0 copy-start.13
  26.8 0.7 copy-done.13
  27.5 0.0 copy-start.14
  27.5 0.7 copy-done.14
  28.1 12.6 %build.1 = (bf16[1024,1024]{1,0:T(8,128)(2,1)S(1)}, bf16[1024,2560]{1,0:T(8,128)(2,1)}, f32[1024,128]{1,0:T(8,128)S(1)}, f32[1024,128]{1,0:T(8,128)S(1)}) custom-call(s32[96]{0:T(128)S(1)} %copy-done.9, s32[96]{0:T(128)S(1)} %copy-done.10, s32[96]{0:T(128)S(1)} %copy-done.11, s32[96]{0:T(128)S(1)} %copy-done.12, s32[96]{0:T(128)S(1)} %copy-done.13, ...), custom_call_target="tpu_custom_call" | custom-call | flops 268435456 | bytes 41943040 | tf_op jit(solution)/shard_map/build/pallas_call | solution.py:253
  40.8 0.0 collective-permute-done.other_ref
  40.8 0.0 copy-start
  40.8 2.5 %copy-done = bf16[1024,2560]{1,0:T(8,128)(2,1)S(1)} copy-done((bf16[1024,2560]{1,0:T(8,128)(2,1)S(1)}, bf16[1024,2560]{1,0:T(8,128)(2,1)}, u32[]{:S(2)}) %copy-start) | copy-done | bytes 5242904
  43.3 0.0 copy-start.3
  43.3 0.0 copy-start.4
  43.3 0.0 copy-start.5
  43.3 0.0 copy-start.6
  43.3 2.5 %mean.1 = (bf16[1024,128]{1,0:T(8,128)(2,1)S(1)}, bf16[32,48,128]{2,1,0:T(8,128)(2,1)S(1)}, bf16[2560,128]{1,0:T(8,128)(2,1)S(1)}) custom-call(bf16[32,48,128]{2,1,0:T(8,128)(2,1)S(1)} %all_to_all.10.own_ref, bf16[32,48,128]{2,1,0:T(8,128)(2,1)S(1)} %collective-permute-done.other_ref, bf16[1024,2560]{1,0:T(8,128)(2,1)S(1)} %copy-done, ...), custom_call_target="tpu_custom_call" | custom-call | tf_op jit(solution)/shard_map/mean/pallas_call | solution.py:286
  45.8 0.0 copy-start.7
  45.8 15.7 %all_to_all.11.own_ref = bf16[32,48,128]{2,1,0:T(8,128)(2,1)S(1)} all-to-all(bf16[32,48,128]{2,1,0:T(8,128)(2,1)S(1)} %get-tuple-element.21), channel_id=1, replica_groups=mesh['nodes'=32] {'nodes'}, dimensions={0} | all-to-all | bytes 786432 | tf_op jit(solution)/shard_map/all_to_all | solution.py:296
  61.6 0.0 collective-permute-start.1
  61.6 0.0 copy-done.3
  61.6 0.0 copy-done.4
  61.6 0.0 copy-done.5
  61.6 0.0 copy-done.6
  61.6 1.5 %own.1 = (f32[1024,256]{1,0:T(8,128)S(1)}, f32[1024,256]{1,0:T(8,128)S(1)}) custom-call(bf16[1024,128]{1,0:T(8,128)(2,1)S(1)} %copy-done.3, bf16[1024,128]{1,0:T(8,128)(2,1)S(1)} %get-tuple-element.23.mean_ref, bf16[1024,1024]{1,0:T(8,128)(2,1)S(1)} %get-tuple-element.24.al_ref, bf16[128,256]{1,0:T(8,128)(2,1)S(1)} %copy-done.4, ...), custom_call_target="tpu_custom_call" | custom-call | flops 536870912 | bytes 20971520 | tf_op jit(solution)/shard_map/own/pallas_call | solution.py:298
  63.1 0.2 collective-permute-done.1.other_ref
  63.3 0.0 copy-done.7
  63.3 6.0 %last.1 = f32[1024,256]{1,0:T(8,128)} custom-call(bf16[32,48,128]{2,1,0:T(8,128)(2,1)S(1)} %all_to_all.11.own_ref, bf16[32,48,128]{2,1,0:T(8,128)(2,1)S(1)} %collective-permute-done.1.other_ref, bf16[2560,128]{1,0:T(8,128)(2,1)S(1)} %get-tuple-element.22.xr_ref, bf16[128,256]{1,0:T(8,128)(2,1)S(1)} %copy-done.4, bf16[128,256]{1,0:T(8,128)(2,1)S(1)} %copy-done.5, ...), custom_call_target="tpu_custom_call" | custom-call | tf_op jit(solution)/shard_map/last/pallas_call | solution.py:312
Async XLA Ops:
  0.8 1.0 %copy-start.1 = (bf16[1024,128]{1,0:T(8,128)(2,1)S(1)}, bf16[1024,128]{1,0:T(8,128)(2,1)}, u32[]{:S(2)}) copy-start(bf16[1024,128]{1,0:T(8,128)(2,1)} %x_ref.5) | copy-start | bytes 786436
  1.7 0.7 copy-start.8
  23.3 17.5 %collective-permute-start = (bf16[32,48,128]{2,1,0:T(8,128)(2,1)S(1)}, bf16[32,48,128]{2,1,0:T(8,128)(2,1)S(1)}, u32[]{:S(2)}, u32[]{:S(2)}) collective-permute-start(bf16[32,48,128]{2,1,0:T(8,128)(2,1)S(1)} %all_to_all.10.own_ref), channel_id=1, source_target_pairs={{0,1},{1,0},{2,3},{3,2},{4,5},{5,4},{6,7},{7,6},{8,9},{9,8},{10,11... | collective-permute-start | bytes 1179656 | tf_op jit(solution)/shard_map/ppermute | solution.py:284
  23.3 1.0 %copy-start.2 = (bf16[1024,128]{1,0:T(8,128)(2,1)S(1)}, bf16[1024,128]{1,0:T(8,128)(2,1)}, u32[]{:S(2)}) copy-start(bf16[1024,128]{1,0:T(8,128)(2,1)} %x_ref.5) | copy-start | bytes 786436
  24.2 0.7 copy-start.9
  24.9 0.7 copy-start.10
  25.5 0.7 copy-start.11
  26.2 0.7 copy-start.12
  26.8 0.7 copy-start.13
  27.5 0.7 copy-start.14
  40.8 2.5 %copy-start = (bf16[1024,2560]{1,0:T(8,128)(2,1)S(1)}, bf16[1024,2560]{1,0:T(8,128)(2,1)}, u32[]{:S(2)}) copy-start(bf16[1024,2560]{1,0:T(8,128)(2,1)} %get-tuple-element.17.ar_ref) | copy-start | bytes 15728644
  43.3 18.3 %copy-start.3 = (bf16[1024,128]{1,0:T(8,128)(2,1)S(1)}, bf16[1024,128]{1,0:T(8,128)(2,1)}, u32[]{:S(2)}) copy-start(bf16[1024,128]{1,0:T(8,128)(2,1)} %x_ref.5) | copy-start | bytes 786436
  43.3 18.3 %copy-start.4 = (bf16[128,256]{1,0:T(8,128)(2,1)S(1)}, bf16[128,256]{1,0:T(8,128)(2,1)}, u32[]{:S(2)}) copy-start(bf16[128,256]{1,0:T(8,128)(2,1)} %self_one.3) | copy-start | bytes 196612
  43.3 18.3 %copy-start.5 = (bf16[128,256]{1,0:T(8,128)(2,1)S(1)}, bf16[128,256]{1,0:T(8,128)(2,1)}, u32[]{:S(2)}) copy-start(bf16[128,256]{1,0:T(8,128)(2,1)} %neigh_one.3) | copy-start | bytes 196612
  43.3 18.3 %copy-start.6 = (bf16[256,256]{1,0:T(8,128)(2,1)S(1)}, bf16[256,256]{1,0:T(8,128)(2,1)}, u32[]{:S(2)}) copy-start(bf16[256,256]{1,0:T(8,128)(2,1)} %self_two.1) | copy-start | bytes 393220
  45.8 17.5 %copy-start.7 = (bf16[256,256]{1,0:T(8,128)(2,1)S(1)}, bf16[256,256]{1,0:T(8,128)(2,1)}, u32[]{:S(2)}) copy-start(bf16[256,256]{1,0:T(8,128)(2,1)} %neigh_two.1) | copy-start | bytes 393220
  61.6 1.7 %collective-permute-start.1 = (bf16[32,48,128]{2,1,0:T(8,128)(2,1)S(1)}, bf16[32,48,128]{2,1,0:T(8,128)(2,1)S(1)}, u32[]{:S(2)}, u32[]{:S(2)}) collective-permute-start(bf16[32,48,128]{2,1,0:T(8,128)(2,1)S(1)} %all_to_all.11.own_ref), channel_id=1, source_target_pairs={{0,1},{1,0},{2,3},{3,2},{4,5},{5,4},{6,7},{7,6},{8,9},{9,8},{10,11... | collective-permute-start | bytes 1179656 | tf_op jit(solution)/shard_map/ppermute | solution.py:310

commit v2 on v1

v2 whole, which is shorter than its diff:
```python
import functools

import jax
import jax.numpy as jnp
from jax import lax
from jax.experimental import pallas as pl
from jax.experimental.pallas import tpu as pltpu
from jax.sharding import PartitionSpec as P

F32 = jnp.float32
BF16 = jnp.bfloat16
MIB = 1024 * 1024


def params(mib):
    return pltpu.CompilerParams(vmem_limit_bytes=mib * MIB)


def whole(memory=pltpu.VMEM):
    return pl.BlockSpec(memory_space=memory)


def dot(a, b):
    return jnp.dot(a, b, preferred_element_type=F32)


def fill_select(lists_ref, hub_ref, sel_ref):
    send_rows, peers = lists_ref.shape
    nodes = sel_ref.shape[1]
    hubs = hub_ref.shape[1]
    place = lax.broadcasted_iota(jnp.int32, (16, nodes), 1).astype(F32)

    def put(start, col):
        sel_ref[start : start + 16, :] = jnp.where(col == place, 1.0, 0.0).astype(BF16)

    lists = lists_ref[...].astype(F32)
    for p in range(peers):
        for c in range(0, send_rows, 16):
            put(p * send_rows + c, lists[c : c + 16, p : p + 1])
    table = jnp.broadcast_to(hub_ref[...].astype(F32), (16, hubs))
    sub = lax.broadcasted_iota(jnp.int32, (16, hubs), 0)
    lane = lax.broadcasted_iota(jnp.int32, (16, hubs), 1)
    for c in range(0, hubs, 16):
        picked = jnp.where(lane == sub + c, table, 0.0)
        put(peers * send_rows + c, jnp.sum(picked, axis=1, keepdims=True))


def fill_send(send_rows, sel, values, send_ref):
    peers = send_ref.shape[0]
    half = (sel.shape[0] - peers * send_rows) // 2
    rows = dot(sel, values).astype(BF16)
    for p in range(peers):
        send_ref[p, 0:send_rows, :] = rows[p * send_rows : (p + 1) * send_rows]
        start = peers * send_rows + half * (p % 2)
        send_ref[p, send_rows : send_rows + half, :] = rows[start : start + half]


def fetch(pairs, sems):
    copies = [pltpu.make_async_copy(src, dst, sems.at[i]) for i, (src, dst) in enumerate(pairs)]
    for copy in copies:
        copy.start()
    return copies


def select_kernel(x_hbm, lists_hbm, hub_hbm, send_ref, x_ref, lists_ref, hub_ref, sel_ref, sems):
    copies = fetch(((lists_hbm, lists_ref), (hub_hbm, hub_ref), (x_hbm, x_ref)), sems)
    copies[0].wait()
    copies[1].wait()
    fill_select(lists_ref, hub_ref, sel_ref)
    copies[2].wait()
    fill_send(lists_ref.shape[0], sel_ref[...], x_ref[...], send_ref)


def build_kernel(
    cols,
    parts,
    chunks,
    ld,
    ls,
    rd,
    rs,
    hd,
    hs,
    x_hbm,
    lt,
    rt,
    ht,
    al_ref,
    ar_hbm,
    inv_hbm,
    agg_ref,
    acc,
    tiles,
    x_ref,
    ar_ref,
    inv_ref,
    tile_sems,
    x_sem,
    out_sems,
):
    part = pl.program_id(0)
    size = acc.shape[1]
    wide = sum(cols)
    blocks = acc.shape[0] // wide
    count = lt.shape[0]
    per = count // chunks
    index = ((ld, ls), (rd, rs), (hd, hs))
    groups = (lt, rt, ht)
    moves = [
        [
            pltpu.make_async_copy(
                groups[g].at[pl.ds(k * per, per)], tiles.at[g, pl.ds(k * per, per)], tile_sems.at[g, k]
            )
            for k in range(chunks)
        ]
        for g in range(3)
    ]
    load_x = pltpu.make_async_copy(x_hbm, x_ref, x_sem)

    @pl.when(part == 0)
    def _():
        for g in range(3):
            for k in range(chunks):
                moves[g][k].start()
        load_x.start()

    def clear(i, _):
        acc[i] = jnp.zeros((size, size), F32)
        return 0

    lax.fori_loop(0, acc.shape[0], clear, 0, unroll=4)

    off = 0
    for g in range(3):
        for k in range(chunks):

            @pl.when(part == 0)
            def _(move=moves[g][k]):
                move.wait()

            def add(i, _, g=g, k=k, off=off):
                t = k * per + i
                d = index[g][0][t]
                slot = d * wide + off + index[g][1][t]
                if parts > 1:
                    low = part * blocks
                    inside = jnp.logical_and(d >= low, d < low + blocks)
                    slot = jnp.where(inside, slot - low * wide, blocks * wide)
                acc[slot] += tiles[g, t].astype(F32)
                return 0

            lax.fori_loop(0, per, add, 0, unroll=4)
        off += cols[g]

    @pl.when(part == 0)
    def _():
        load_x.wait()

    def leave(b):
        rows = pl.ds(pl.multiple_of(b * size, size), size)
        there = pl.ds(pl.multiple_of((part * blocks + b) * size, size), size)
        return (
            pltpu.make_async_copy(ar_ref.at[rows], ar_hbm.at[there], out_sems.at[0, b]),
            pltpu.make_async_copy(inv_ref.at[rows], inv_hbm.at[there], out_sems.at[1, b]),
        )

    def finish(b, _):
        rows = pl.ds(pl.multiple_of(b * size, size), size)
        total = jnp.zeros((size, size), F32)
        for c in range(wide):
            tile = acc[b * wide + c]
            total += tile
            ref, at = (al_ref, c) if c < cols[0] else (ar_ref, c - cols[0])
            ref[rows, at * size : (at + 1) * size] = tile.astype(BF16)
        deg = 1.0 + jnp.sum(total, axis=1, keepdims=True)
        inv_ref[rows, :] = jnp.broadcast_to(1.0 / deg, (size, size))
        for copy in leave(b):
            copy.start()
        agg_ref[rows, :] = dot(al_ref[rows, :], x_ref[...])
        return 0

    lax.fori_loop(0, blocks, finish, 0)

    def end(b, _):
        for copy in leave(b):
            copy.wait()
        return 0

    lax.fori_loop(0, blocks, end, 0)


def assemble(send_rows, own_ref, other_ref, dest_ref, lanes):
    peers, per = own_ref.shape[:2]
    half = per - send_rows
    mine = lax.rem(lax.axis_index("nodes"), 2)
    base = peers * send_rows
    for o in range(peers):
        dest_ref[o * send_rows : (o + 1) * send_rows, lanes] = own_ref[o, 0:send_rows, :]
        for ref, h in ((own_ref, mine), (other_ref, 1 - mine)):
            at = pl.multiple_of(base + o * 2 * half + h * half, half)
            dest_ref[pl.ds(at, half), lanes] = ref[o, send_rows:per, :]


def stage_kernel(lists_hbm, hub_hbm, _, *refs):
    pairs = len(refs) // 2 - 2
    sources, targets = refs[:pairs], refs[pairs : 2 * pairs]
    sel_ref, lists_ref, hub_ref, sems = refs[2 * pairs :]
    copies = fetch(((lists_hbm, lists_ref), (hub_hbm, hub_ref), *zip(sources, targets)), sems)
    copies[0].wait()
    copies[1].wait()
    fill_select(lists_ref, hub_ref, sel_ref)
    for copy in copies[2:]:
        copy.wait()


def cuts_of(rows, cuts):
    return [slice(k * rows // cuts, (k + 1) * rows // cuts) for k in range(cuts)]


def mean_kernel(
    send_rows, parts, own_ref, other_ref, agg_ref, a_ref, inv_ref, sel_ref, mean_ref, send_ref, xr_ref
):
    part = pl.program_id(0)
    rows = a_ref.shape[0]

    @pl.when(part == 0)
    def _():
        assemble(send_rows, own_ref, other_ref, xr_ref, slice(None))

    for at in cuts_of(rows, 4):
        agg = agg_ref[at, :] + dot(a_ref[at, :], xr_ref[...])
        there = pl.ds(pl.multiple_of(part * rows + at.start, rows // 4), rows // 4)
        mean_ref[there, :] = (agg * inv_ref[at, :]).astype(BF16)

    @pl.when(part == parts - 1)
    def _():
        fill_send(send_rows, sel_ref[...], mean_ref[...], send_ref)


def own_kernel(x_ref, mean_ref, a_ref, self_one, neigh_one, self_two, agg_ref, part_ref, first):
    part = pl.program_id(0)
    rows = a_ref.shape[0]

    @pl.when(part == 0)
    def _():
        total = dot(x_ref[...], self_one[...]) + dot(mean_ref[...], neigh_one[...])
        first[...] = jnp.maximum(total, 0.0).astype(BF16)

    for at in cuts_of(rows, 4):
        agg_ref[at, :] = dot(a_ref[at, :], first[...])
    at = pl.ds(pl.multiple_of(part * rows, rows), rows)
    part_ref[...] = dot(first[at, :], self_two[...])


def last_kernel(
    send_rows,
    own_one,
    other_one,
    own_two,
    other_two,
    agg_ref,
    part_ref,
    inv_ref,
    a_ref,
    self_one,
    neigh_one,
    neigh_two,
    out_hbm,
    both,
    weight,
    first,
    out_ref,
    sems,
):
    part = pl.program_id(0)
    rows = a_ref.shape[0]
    width = both.shape[1] // 2

    @pl.when(part == 0)
    def _():
        assemble(send_rows, own_one, other_one, both, slice(0, width))
        assemble(send_rows, own_two, other_two, both, slice(width, 2 * width))
        weight[0:width, :] = self_one[...]
        weight[width : 2 * width, :] = neigh_one[...]
        first[...] = jnp.maximum(dot(both[...], weight[...]), 0.0).astype(BF16)

    outs = []
    for k, at in enumerate(cuts_of(rows, 4)):
        agg = agg_ref[at, :] + dot(a_ref[at, :], first[...])
        inv = inv_ref[at, :]
        inv = jnp.concatenate([inv] * (agg.shape[1] // inv.shape[1]), axis=1)
        mean = (agg * inv).astype(BF16)
        out_ref[at, :] = jnp.maximum(part_ref[at, :] + dot(mean, neigh_two[...]), 0.0)
        there = pl.ds(pl.multiple_of(part * rows + at.start, rows // 4), rows // 4)
        outs.append(pltpu.make_async_copy(out_ref.at[at], out_hbm.at[there], sems.at[k]))
        outs[k].start()
    for copy in outs:
        copy.wait()


def per_device(
    features,
    send_lists,
    hub_rows,
    local_tiles,
    local_dst,
    local_src,
    remote_tiles,
    remote_dst,
    remote_src,
    hub_tiles,
    hub_dst,
    hub_src,
    self_one,
    neigh_one,
    self_two,
    neigh_two,
):
    nodes, f_in = features.shape
    hid = self_one.shape[1]
    tiles, size = local_tiles.shape[:2]
    _, peers, send_rows = send_lists.shape
    hubs = hub_rows.shape[0]
    per = send_rows + hubs // 2
    far = peers * (send_rows + hubs)
    cols = (nodes // size, peers * send_rows // size, peers * hubs // size)
    wide = sum(cols)
    blocks = nodes // size
    parts = 1
    while blocks * wide * size * size * 4 > parts * 16 * MIB:
        parts *= 2
    rows = nodes // parts
    spare = 0 if parts == 1 else 1
    swap = [(i, i ^ 1) for i in range(peers)]
    sds = jax.ShapeDtypeStruct
    vm = whole()
    hbm = whole(pltpu.HBM)

    def split(width):
        return vm if parts == 1 else pl.BlockSpec((rows, width), lambda i, *_: (i, 0))

    dma = pltpu.SemaphoreType.DMA

    def in_hbm(*arrays):
        return [pltpu.with_memory_space_constraint(a, pltpu.HBM) for a in arrays]

    def kept(shape, dtype):
        return sds(shape, dtype) if parts > 1 else pltpu.VMEM(shape, dtype)

    lists = send_lists[0].T
    hub_row = hub_rows.reshape(1, hubs)
    chosen = peers * send_rows + hubs
    tables = [pltpu.VMEM((send_rows, peers), jnp.int32), pltpu.VMEM((1, hubs), jnp.int32)]
    send = pl.pallas_call(
        select_kernel,
        out_shape=kept((peers, per, f_in), BF16),
        in_specs=[hbm] * 3,
        out_specs=vm,
        scratch_shapes=[pltpu.VMEM((nodes, f_in), BF16), *tables, pltpu.VMEM((chosen, nodes), BF16), dma((3,))],
        compiler_params=params(16),
        name="select",
    )(*in_hbm(features, lists, hub_row))

    got = lax.all_to_all(send, "nodes", split_axis=0, concat_axis=0, tiled=True)

    chunks = 2
    a_local, a_far, inv, agg = pl.pallas_call(
        functools.partial(build_kernel, cols, parts, chunks),
        out_shape=(
            kept((nodes, nodes), BF16),
            pltpu.HBM((nodes, far), BF16),
            pltpu.HBM((nodes, size), F32),
            kept((nodes, f_in), F32),
        ),
        grid=(parts,),
        in_specs=[whole(pltpu.SMEM)] * 6 + [hbm] * 4,
        out_specs=(split(nodes), hbm, hbm, split(f_in)),
        scratch_shapes=[
            pltpu.VMEM((blocks // parts * wide + spare, size, size), F32),
            pltpu.VMEM((3, tiles, size, size), BF16),
            pltpu.VMEM((nodes, f_in), BF16),
            pltpu.VMEM((rows, far), BF16),
            pltpu.VMEM((rows, size), F32),
            dma((3, chunks)),
            dma(()),
            dma((2, blocks // parts)),
        ],
        compiler_params=params(36 if parts == 1 else 48),
        cost_estimate=pl.CostEstimate(flops=2 * nodes * nodes * f_in, bytes_accessed=40 * MIB, transcendentals=0),
        name="build",
    )(
        *in_hbm(local_dst, local_src, remote_dst, remote_src, hub_dst, hub_src),
        *in_hbm(features, local_tiles, remote_tiles, hub_tiles),
    )
    got, a_local, a_far, inv, agg = lax.optimization_barrier((got, a_local, a_far, inv, agg))

    other = lax.ppermute(got, "nodes", swap)

    staged = (a_far, inv) if parts == 1 else ()
    *moved, sel = pl.pallas_call(
        stage_kernel,
        out_shape=(*(kept(x.shape, x.dtype) for x in staged), kept((chosen, nodes), BF16)),
        in_specs=[hbm, hbm, whole(pl.ANY)] + [hbm] * len(staged),
        out_specs=(vm,) * (1 + len(staged)),
        scratch_shapes=[*tables, dma((2 + len(staged),))],
        compiler_params=params(8 if parts == 1 else 16),
        cost_estimate=pl.CostEstimate(flops=0, bytes_accessed=8 * MIB, transcendentals=0),
        name="stage",
    )(*in_hbm(lists, hub_row), got, *in_hbm(*staged))
    if staged:
        a_far, inv = moved

    mean, send = pl.pallas_call(
        functools.partial(mean_kernel, send_rows, parts),
        out_shape=(sds((nodes, f_in), BF16), sds(send.shape, BF16)),
        grid=(parts,),
        in_specs=[vm] * 2 + [split(f_in), split(far), split(size), vm],
        out_specs=(vm, vm),
        scratch_shapes=[pltpu.VMEM((far, f_in), BF16)],
        compiler_params=params(8 if parts == 1 else 48),
        name="mean",
    )(got, other, agg, a_far, inv, sel)

    got_two = lax.all_to_all(send, "nodes", split_axis=0, concat_axis=0, tiled=True)
    got_two, mean = lax.optimization_barrier((got_two, mean))
    other_two = lax.ppermute(got_two, "nodes", swap)

    agg, part = pl.pallas_call(
        own_kernel,
        out_shape=(sds((nodes, hid), F32), sds((nodes, hid), F32)),
        grid=(parts,),
        in_specs=[vm, vm, split(nodes), vm, vm, vm],
        out_specs=(split(hid), split(hid)),
        scratch_shapes=[pltpu.VMEM((nodes, hid), BF16)],
        compiler_params=params(16),
        cost_estimate=pl.CostEstimate(flops=2 * nodes * nodes * hid, bytes_accessed=8 * MIB, transcendentals=0),
        name="own",
    )(features, mean, a_local, self_one, neigh_one, self_two)

    return pl.pallas_call(
        functools.partial(last_kernel, send_rows),
        out_shape=sds((nodes, hid), F32),
        grid=(parts,),
        in_specs=[vm] * 4 + [split(hid), split(hid), split(size), split(far)] + [vm] * 3,
        out_specs=hbm,
        scratch_shapes=[
            pltpu.VMEM((far, 2 * f_in), BF16),
            pltpu.VMEM((2 * f_in, hid), BF16),
            pltpu.VMEM((far, hid), BF16),
            pltpu.VMEM((rows, hid), F32),
            dma((4,)),
        ],
        compiler_params=params(16 if parts == 1 else 56),
        name="last",
    )(got, other, got_two, other_two, agg, part, inv, a_far, self_one, neigh_one, neigh_two)


def solution(mesh):
    placed = (
        P("nodes", None),
        P("nodes", None, None),
        P("nodes"),
        P("nodes", None, None),
        P("nodes"),
        P("nodes"),
        P("nodes", None, None),
        P("nodes"),
        P("nodes"),
        P("nodes", None, None),
        P("nodes"),
        P("nodes"),
        P(),
        P(),
        P(),
        P(),
    )
    return jax.shard_map(
        per_device, mesh=mesh, in_specs=placed, out_specs=P("nodes", None), check_vma=False
    )
```

time: 69.8 us -> 49.4 us (0.71)
  blocking collectives: 36 us -> 15.7 us
  local copies, waits for them, and re-layouts: 9.76 us -> 0.03 us
  starting transfers between devices: 0.01 us -> 7.31 us
  waiting for transfers between devices: 0.16 us -> 5.33 us
  Pallas kernels: 23.3 us -> 20.5 us
    all_to_all x2 -> x1, blocking collectives: 36 us -> 15.7 us  [per_device(): lax.all_to_all(send, 'nodes', split_axis=0, concat_axis=0, tiled=True)]
    unnamed x31 -> x10, local copies, waits for them, and re-layouts: 9.76 us -> 0.03 us
    all_to_all x0 -> x1, starting transfers between devices: none -> 7.3 us  [per_device(): got = lax.all_to_all(send, 'nodes', split_axis=0, concat_axis=0, tiled=True)]
    all_to_all x0 -> x1, waiting for transfers between devices: none -> 4.92 us  [per_device(): got = lax.all_to_all(send, 'nodes', split_axis=0, concat_axis=0, tiled=True)]
    pallas_call x1, Pallas kernels: 6 us -> 4.2 us  [per_device(): pl.pallas_call(functools.partial(last_kernel, send_rows), out_shape=sds((...]
    pallas_call x2 -> x3, Pallas kernels: 13.2 us -> 13.2 us  [the longest x1 8.25 us: per_device(): pl.pallas_call(functools.partial(build_kernel, cols, parts, chunks), out_...]
  transfers between devices with their start and end apart: 2 -> 3, of which waited for: 1 -> 2; matrix products, arithmetic and copies ran while one was open for 0% -> 0% of each run, Pallas kernels for 20% -> 25%
where the time goes in v2:
time: 49.4 us; the launch traced here: 49 us
  Pallas kernels  20.5 us (41%)
  blocking collectives  15.7 us (32%)
  starting transfers between devices  7.31 us (15%)
  waiting for transfers between devices  5.33 us (11%)
    all_to_all x1, blocking collectives, per_device(): lax.all_to_all(send, 'nodes', split_axis=0, concat_axis=0, tiled=True)  15.7 us
    pallas_call x1, Pallas kernels, per_device(): pl.pallas_call(functools.partial(build_kernel, cols, parts, chunks), out_...  8.25 us
    all_to_all x1, starting transfers between devices, per_device(): got = lax.all_to_all(send, 'nodes', split_axis=0, concat_axis=0, tiled=True)  7.3 us
    all_to_all x1, waiting for transfers between devices, per_device(): got = lax.all_to_all(send, 'nodes', split_axis=0, concat_axis=0, tiled=True)  4.92 us
    pallas_call x1, Pallas kernels, per_device(): pl.pallas_call(functools.partial(last_kernel, send_rows), out_shape=sds((...  4.2 us
    pallas_call x1, Pallas kernels, per_device(): pl.pallas_call(stage_kernel, out_shape=(*(kept(x.shape, x.dtype) for x in...  2.66 us
    pallas_call x1, Pallas kernels, per_device(): pl.pallas_call(select_kernel, out_shape=kept((peers, per, f_in), BF16), i...  2.26 us
    pallas_call x1, Pallas kernels, per_device(): pl.pallas_call(functools.partial(mean_kernel, send_rows, parts), out_shap...  1.88 us
  transfers between devices with their start and end apart: 3, of which 2 were waited for; matrix products, arithmetic and copies ran while one was open for 0% of the time, Pallas kernels for 25%

profile of v2, /device:TPU:0, one launch (start us, length us, event | category | flops | bytes accessed | tf_op | source)
XLA Modules:
  0.0 49.0 jit_solution(5098259571181412848)
XLA Ops:
  0.0 2.3 %select.1 = bf16[32,48,128]{2,1,0:T(8,128)(2,1)} custom-call(bf16[1024,128]{1,0:T(8,128)(2,1)} %x_ref.1, s32[16,32]{1,0:T(8,128)} %bitcast.4, s32[1,64]{1,0:T(1,128)} %bitcast.6), custom_call_target="tpu_custom_call" | custom-call | tf_op jit(solution)/shard_map/select/pallas_call | solution.py:354
  2.3 7.3 %all-to-all-start = ((bf16[32,48,128]{2,1,0:T(8,128)(2,1)}), bf16[32,48,128]{2,1,0:T(8,128)(2,1)S(1)}, u32[]{:S(2)}, u32[]{:S(2)}) async-start(bf16[32,48,128]{2,1,0:T(8,128)(2,1)} %select.1), calls=%async_computation | async-start | bytes 786432 | tf_op jit(solution)/shard_map/all_to_all | solution.py:364
  9.6 8.3 %build.1 = (bf16[1024,1024]{1,0:T(8,128)(2,1)S(1)}, bf16[1024,2560]{1,0:T(8,128)(2,1)}, f32[1024,128]{1,0:T(8,128)}, f32[1024,128]{1,0:T(8,128)S(1)}) custom-call(s32[96]{0:T(128)} %ld.1, s32[96]{0:T(128)} %ls.1, s32[96]{0:T(128)} %rd.1, s32[96]{0:T(128)} %rs.1, s32[96]{0:T(128)} %hd.1, s32[96]{0:T(128)} %hs.1, bf16[1024,128]{1,0:T(8,128)(2,1)} %x_ref.1, ...), custom_call_target="tpu_custom_call" | custom-call | flops 268435456 | bytes 41943040 | tf_op jit(solution)/shard_map/build/pallas_call | solution.py:367
  17.8 4.9 %all-to-all-done._.own_ref.own_one = bf16[32,48,128]{2,1,0:T(8,128)(2,1)S(1)} async-done(((bf16[32,48,128]{2,1,0:T(8,128)(2,1)}), bf16[32,48,128]{2,1,0:T(8,128)(2,1)S(1)}, u32[]{:S(2)}, u32[]{:S(2)}) %all-to-all-start) | async-done | bytes 393248 | tf_op jit(solution)/shard_map/all_to_all | solution.py:364
  22.8 0.0 collective-permute-start
  22.8 2.7 %stage.1 = (bf16[1024,2560]{1,0:T(8,128)(2,1)S(1)}, f32[1024,128]{1,0:T(8,128)S(1)}, bf16[576,1024]{1,0:T(8,128)(2,1)S(1)}) custom-call(s32[16,32]{1,0:T(8,128)} %bitcast.5, s32[1,64]{1,0:T(1,128)} %bitcast.7, bf16[32,48,128]{2,1,0:T(8,128)(2,1)S(1)} %all-to-all-done._.own_ref.own_one, bf16[1024,2560]{1,0:T(8,128)(2,1)} %get-tuple-element.29.refs_0_, ...), custom_call_target="tpu_custom_call" | custom-call | bytes 8388608 | tf_op jit(solution)/shard_map/stage/pallas_call | solution.py:400
  25.4 0.0 collective-permute-done.other_ref.other_one
  25.4 0.0 copy-start
  25.4 0.0 copy-start.1
  25.5 0.0 copy-start.2
  25.5 0.0 copy-start.4
  25.5 1.9 %mean.1 = (bf16[1024,128]{1,0:T(8,128)(2,1)S(1)}, bf16[32,48,128]{2,1,0:T(8,128)(2,1)S(1)}) custom-call(bf16[32,48,128]{2,1,0:T(8,128)(2,1)S(1)} %all-to-all-done._.own_ref.own_one, bf16[32,48,128]{2,1,0:T(8,128)(2,1)S(1)} %collective-permute-done.other_ref.other_one, f32[1024,128]{1,0:T(8,128)S(1)} %get-tuple-element.28.agg_ref, ...), custom_call_target="tpu_custom_call" | custom-call | tf_op jit(solution)/shard_map/mean/pallas_call | solution.py:413
  27.4 0.0 copy-start.3
  27.4 15.7 %all_to_all.10.own_two = bf16[32,48,128]{2,1,0:T(8,128)(2,1)S(1)} all-to-all(bf16[32,48,128]{2,1,0:T(8,128)(2,1)S(1)} %get-tuple-element.34), channel_id=1, replica_groups=mesh['nodes'=32] {'nodes'}, dimensions={0} | all-to-all | bytes 786432 | tf_op jit(solution)/shard_map/all_to_all | solution.py:424
  43.1 0.0 collective-permute-start.1
  43.1 0.0 copy-done
  43.1 0.0 copy-done.1
  43.1 0.0 copy-done.2
  43.1 0.0 copy-done.4
  43.1 1.3 %own.1 = (f32[1024,256]{1,0:T(8,128)S(1)}, f32[1024,256]{1,0:T(8,128)S(1)}) custom-call(bf16[1024,128]{1,0:T(8,128)(2,1)S(1)} %copy-done, bf16[1024,128]{1,0:T(8,128)(2,1)S(1)} %get-tuple-element.37.mean_ref, bf16[1024,1024]{1,0:T(8,128)(2,1)S(1)} %get-tuple-element.38.a_ref, bf16[128,256]{1,0:T(8,128)(2,1)S(1)} %copy-done.1, ...), custom_call_target="tpu_custom_call" | custom-call | flops 536870912 | bytes 8388608 | tf_op jit(solution)/shard_map/own/pallas_call | solution.py:428
  44.4 0.4 collective-permute-done.1.other_two
  44.8 0.0 copy-done.3
  44.8 4.2 %last.1 = f32[1024,256]{1,0:T(8,128)} custom-call(bf16[32,48,128]{2,1,0:T(8,128)(2,1)S(1)} %all-to-all-done._.own_ref.own_one, bf16[32,48,128]{2,1,0:T(8,128)(2,1)S(1)} %collective-permute-done.other_ref.other_one, bf16[32,48,128]{2,1,0:T(8,128)(2,1)S(1)} %all_to_all.10.own_two, bf16[32,48,128]{2,1,0:T(8,128)(2,1)S(1)} %collective-permute-done.1.other_two, ...), custom_call_target="tpu_custom_call" | custom-call | tf_op jit(solution)/shard_map/last/pallas_call | solution.py:440
Async XLA Ops:
  2.3 20.5 %all-to-all-start = ((bf16[32,48,128]{2,1,0:T(8,128)(2,1)}), bf16[32,48,128]{2,1,0:T(8,128)(2,1)S(1)}, u32[]{:S(2)}, u32[]{:S(2)}) async-start(bf16[32,48,128]{2,1,0:T(8,128)(2,1)} %select.1), calls=%async_computation | async-start | bytes 786432 | tf_op jit(solution)/shard_map/all_to_all | solution.py:364
  22.8 2.7 %collective-permute-start = (bf16[32,48,128]{2,1,0:T(8,128)(2,1)S(1)}, bf16[32,48,128]{2,1,0:T(8,128)(2,1)S(1)}, u32[]{:S(2)}, u32[]{:S(2)}) collective-permute-start(bf16[32,48,128]{2,1,0:T(8,128)(2,1)S(1)} %all-to-all-done._.own_ref.own_one), channel_id=1, source_target_pairs={{0,1},{1,0},{2,3},{3,2},{4,5},{5,4},{6,7},{7,6},{8,9},{9,8},{10,11... | collective-permute-start | bytes 1179656 | tf_op jit(solution)/shard_map/ppermute | solution.py:397
  25.4 17.7 %copy-start = (bf16[1024,128]{1,0:T(8,128)(2,1)S(1)}, bf16[1024,128]{1,0:T(8,128)(2,1)}, u32[]{:S(2)}) copy-start(bf16[1024,128]{1,0:T(8,128)(2,1)} %x_ref.1) | copy-start | bytes 786436
  25.4 17.7 %copy-start.1 = (bf16[128,256]{1,0:T(8,128)(2,1)S(1)}, bf16[128,256]{1,0:T(8,128)(2,1)}, u32[]{:S(2)}) copy-start(bf16[128,256]{1,0:T(8,128)(2,1)} %self_one.3) | copy-start | bytes 196612
  25.5 17.7 %copy-start.2 = (bf16[128,256]{1,0:T(8,128)(2,1)S(1)}, bf16[128,256]{1,0:T(8,128)(2,1)}, u32[]{:S(2)}) copy-start(bf16[128,256]{1,0:T(8,128)(2,1)} %neigh_one.3) | copy-start | bytes 196612
  25.5 17.7 %copy-start.4 = (bf16[256,256]{1,0:T(8,128)(2,1)S(1)}, bf16[256,256]{1,0:T(8,128)(2,1)}, u32[]{:S(2)}) copy-start(bf16[256,256]{1,0:T(8,128)(2,1)} %self_two.1) | copy-start | bytes 393220
  27.4 17.5 %copy-start.3 = (bf16[256,256]{1,0:T(8,128)(2,1)S(1)}, bf16[256,256]{1,0:T(8,128)(2,1)}, u32[]{:S(2)}) copy-start(bf16[256,256]{1,0:T(8,128)(2,1)} %neigh_two.1) | copy-start | bytes 393220
  43.1 1.7 %collective-permute-start.1 = (bf16[32,48,128]{2,1,0:T(8,128)(2,1)S(1)}, bf16[32,48,128]{2,1,0:T(8,128)(2,1)S(1)}, u32[]{:S(2)}, u32[]{:S(2)}) collective-permute-start(bf16[32,48,128]{2,1,0:T(8,128)(2,1)S(1)} %all_to_all.10.own_two), channel_id=1, source_target_pairs={{0,1},{1,0},{2,3},{3,2},{4,5},{5,4},{6,7},{7,6},{8,9},{9,8},{10,11... | collective-permute-start | bytes 1179656 | tf_op jit(solution)/shard_map/ppermute | solution.py:426

commit v3 on v2

--- a/solution.py
+++ b/solution.py
@@ -85,13 +85,15 @@
     lt,
     rt,
     ht,
-    al_ref,
+    al_hbm,
     ar_hbm,
     inv_hbm,
+    near_ref,
     agg_ref,
     acc,
     tiles,
     x_ref,
+    al_ref,
     ar_ref,
     inv_ref,
     tile_sems,
@@ -101,6 +103,7 @@
     part = pl.program_id(0)
     size = acc.shape[1]
     wide = sum(cols)
+    near = wide - near_ref.shape[1] // size
     blocks = acc.shape[0] // wide
     count = lt.shape[0]
     per = count // chunks
@@ -162,6 +165,7 @@
         return (
             pltpu.make_async_copy(ar_ref.at[rows], ar_hbm.at[there], out_sems.at[0, b]),
             pltpu.make_async_copy(inv_ref.at[rows], inv_hbm.at[there], out_sems.at[1, b]),
+            pltpu.make_async_copy(al_ref.at[rows], al_hbm.at[there], out_sems.at[2, b]),
         )
 
     def finish(b, _):
@@ -170,7 +174,12 @@
         for c in range(wide):
             tile = acc[b * wide + c]
             total += tile
-            ref, at = (al_ref, c) if c < cols[0] else (ar_ref, c - cols[0])
+            if c < cols[0]:
+                ref, at = al_ref, c
+            elif c < near:
+                ref, at = ar_ref, c - cols[0]
+            else:
+                ref, at = near_ref, c - near
             ref[rows, at * size : (at + 1) * size] = tile.astype(BF16)
         deg = 1.0 + jnp.sum(total, axis=1, keepdims=True)
         inv_ref[rows, :] = jnp.broadcast_to(1.0 / deg, (size, size))
@@ -213,12 +222,17 @@
         copy.wait()
 
 
+def far_dot(a_ref, near_ref, at, values_ref):
+    split = a_ref.shape[1]
+    return dot(a_ref[at, :], values_ref[0:split, :]) + dot(near_ref[at, :], values_ref[split:, :])
+
+
 def cuts_of(rows, cuts):
     return [slice(k * rows // cuts, (k + 1) * rows // cuts) for k in range(cuts)]
 
 
 def mean_kernel(
-    send_rows, parts, own_ref, other_ref, agg_ref, a_ref, inv_ref, sel_ref, mean_ref, send_ref, xr_ref
+    send_rows, parts, own_ref, other_ref, agg_ref, a_ref, near_ref, inv_ref, sel_ref, mean_ref, send_ref, xr_ref
 ):
     part = pl.program_id(0)
     rows = a_ref.shape[0]
@@ -228,7 +242,7 @@
         assemble(send_rows, own_ref, other_ref, xr_ref, slice(None))
 
     for at in cuts_of(rows, 4):
-        agg = agg_ref[at, :] + dot(a_ref[at, :], xr_ref[...])
+        agg = agg_ref[at, :] + far_dot(a_ref, near_ref, at, xr_ref)
         there = pl.ds(pl.multiple_of(part * rows + at.start, rows // 4), rows // 4)
         mean_ref[there, :] = (agg * inv_ref[at, :]).astype(BF16)
 
@@ -262,6 +276,7 @@
     part_ref,
     inv_ref,
     a_ref,
+    near_ref,
     self_one,
     neigh_one,
     neigh_two,
@@ -269,6 +284,7 @@
     both,
     weight,
     first,
+    mean_ref,
     out_ref,
     sems,
 ):
@@ -284,13 +300,14 @@
         weight[width : 2 * width, :] = neigh_one[...]
         first[...] = jnp.maximum(dot(both[...], weight[...]), 0.0).astype(BF16)
 
+    for at in cuts_of(rows, 4):
+        agg = agg_ref[at, :] + far_dot(a_ref, near_ref, at, first)
+        inv = inv_ref[at, :]
+        inv = jnp.concatenate([inv] * (agg.shape[1] // inv.shape[1]), axis=1)
+        mean_ref[at, :] = (agg * inv).astype(BF16)
     outs = []
     for k, at in enumerate(cuts_of(rows, 4)):
-        agg = agg_ref[at, :] + dot(a_ref[at, :], first[...])
-        inv = inv_ref[at, :]
-        inv = jnp.concatenate([inv] * (agg.shape[1] // inv.shape[1]), axis=1)
-        mean = (agg * inv).astype(BF16)
-        out_ref[at, :] = jnp.maximum(part_ref[at, :] + dot(mean, neigh_two[...]), 0.0)
+        out_ref[at, :] = jnp.maximum(part_ref[at, :] + dot(mean_ref[at, :], neigh_two[...]), 0.0)
         there = pl.ds(pl.multiple_of(part * rows + at.start, rows // 4), rows // 4)
         outs.append(pltpu.make_async_copy(out_ref.at[at], out_hbm.at[there], sems.at[k]))
         outs[k].start()
@@ -364,26 +381,29 @@
     got = lax.all_to_all(send, "nodes", split_axis=0, concat_axis=0, tiled=True)
 
     chunks = 2
-    a_local, a_far, inv, agg = pl.pallas_call(
+    near = nodes
+    a_local, a_far, inv, a_near, agg = pl.pallas_call(
         functools.partial(build_kernel, cols, parts, chunks),
         out_shape=(
-            kept((nodes, nodes), BF16),
-            pltpu.HBM((nodes, far), BF16),
+            pltpu.HBM((nodes, nodes), BF16),
+            pltpu.HBM((nodes, far - near), BF16),
             pltpu.HBM((nodes, size), F32),
+            kept((nodes, near), BF16),
             kept((nodes, f_in), F32),
         ),
         grid=(parts,),
         in_specs=[whole(pltpu.SMEM)] * 6 + [hbm] * 4,
-        out_specs=(split(nodes), hbm, hbm, split(f_in)),
+        out_specs=(hbm, hbm, hbm, split(near), split(f_in)),
         scratch_shapes=[
             pltpu.VMEM((blocks // parts * wide + spare, size, size), F32),
             pltpu.VMEM((3, tiles, size, size), BF16),
             pltpu.VMEM((nodes, f_in), BF16),
-            pltpu.VMEM((rows, far), BF16),
+            pltpu.VMEM((rows, nodes), BF16),
+            pltpu.VMEM((rows, far - near), BF16),
             pltpu.VMEM((rows, size), F32),
             dma((3, chunks)),
             dma(()),
-            dma((2, blocks // parts)),
+            dma((3, blocks // parts)),
         ],
         compiler_params=params(36 if parts == 1 else 48),
         cost_estimate=pl.CostEstimate(flops=2 * nodes * nodes * f_in, bytes_accessed=40 * MIB, transcendentals=0),
@@ -392,7 +412,8 @@
         *in_hbm(local_dst, local_src, remote_dst, remote_src, hub_dst, hub_src),
         *in_hbm(features, local_tiles, remote_tiles, hub_tiles),
     )
-    got, a_local, a_far, inv, agg = lax.optimization_barrier((got, a_local, a_far, inv, agg))
+    built = (got, a_local, a_far, inv, a_near, agg)
+    got, a_local, a_far, inv, a_near, agg = lax.optimization_barrier(built)
 
     other = lax.ppermute(got, "nodes", swap)
 
@@ -414,12 +435,12 @@
         functools.partial(mean_kernel, send_rows, parts),
         out_shape=(sds((nodes, f_in), BF16), sds(send.shape, BF16)),
         grid=(parts,),
-        in_specs=[vm] * 2 + [split(f_in), split(far), split(size), vm],
+        in_specs=[vm] * 2 + [split(f_in), split(far - near), split(near), split(size), vm],
         out_specs=(vm, vm),
         scratch_shapes=[pltpu.VMEM((far, f_in), BF16)],
         compiler_params=params(8 if parts == 1 else 48),
         name="mean",
-    )(got, other, agg, a_far, inv, sel)
+    )(got, other, agg, a_far, a_near, inv, sel)
 
     got_two = lax.all_to_all(send, "nodes", split_axis=0, concat_axis=0, tiled=True)
     got_two, mean = lax.optimization_barrier((got_two, mean))
@@ -441,18 +462,19 @@
         functools.partial(last_kernel, send_rows),
         out_shape=sds((nodes, hid), F32),
         grid=(parts,),
-        in_specs=[vm] * 4 + [split(hid), split(hid), split(size), split(far)] + [vm] * 3,
+        in_specs=[vm] * 4 + [split(hid), split(hid), split(size), split(far - near), split(near)] + [vm] * 3,
         out_specs=hbm,
         scratch_shapes=[
             pltpu.VMEM((far, 2 * f_in), BF16),
             pltpu.VMEM((2 * f_in, hid), BF16),
             pltpu.VMEM((far, hid), BF16),
+            pltpu.VMEM((rows, hid), BF16),
             pltpu.VMEM((rows, hid), F32),
             dma((4,)),
         ],
         compiler_params=params(16 if parts == 1 else 56),
         name="last",
-    )(got, other, got_two, other_two, agg, part, inv, a_far, self_one, neigh_one, neigh_two)
+    )(got, other, got_two, other_two, agg, part, inv, a_far, a_near, self_one, neigh_one, neigh_two)
 
 
 def solution(mesh):

time: 49.4 us -> 48 us (0.972)
  Pallas kernels: 20.5 us -> 19.1 us
    pallas_call x1, Pallas kernels: 4.2 us -> 3.29 us  [per_device(): pl.pallas_call(functools.partial(last_kernel, send_rows), out_shape=sds((...]
    pallas_call x1, Pallas kernels: 2.66 us -> 2.05 us  [per_device(): pl.pallas_call(stage_kernel, out_shape=(*(kept(x.shape, x.dtype) for x in...]
  transfers between devices with their start and end apart: 3 -> 3, of which waited for: 2 -> 2; matrix products, arithmetic and copies ran while one was open for 0% -> 0% of each run, Pallas kernels for 25% -> 24%
where the time goes in v3:
time: 48 us; the launch traced here: 47.6 us
  Pallas kernels  19.1 us (40%)
  blocking collectives  15.7 us (33%)
  starting transfers between devices  7.31 us (15%)
  waiting for transfers between devices  5.25 us (11%)
    all_to_all x1, blocking collectives, per_device(): lax.all_to_all(send, 'nodes', split_axis=0, concat_axis=0, tiled=True)  15.7 us
    pallas_call x1, Pallas kernels, per_device(): pl.pallas_call(functools.partial(build_kernel, cols, parts, chunks), out_...  8.32 us
    all_to_all x1, starting transfers between devices, per_device(): got = lax.all_to_all(send, 'nodes', split_axis=0, concat_axis=0, tiled=True)  7.3 us
    all_to_all x1, waiting for transfers between devices, per_device(): got = lax.all_to_all(send, 'nodes', split_axis=0, concat_axis=0, tiled=True)  4.84 us
    pallas_call x1, Pallas kernels, per_device(): pl.pallas_call(functools.partial(last_kernel, send_rows), out_shape=sds((...  3.29 us
    pallas_call x1, Pallas kernels, per_device(): pl.pallas_call(select_kernel, out_shape=kept((peers, per, f_in), BF16), i...  2.25 us
    pallas_call x1, Pallas kernels, per_device(): pl.pallas_call(stage_kernel, out_shape=(*(kept(x.shape, x.dtype) for x in...  2.05 us
    pallas_call x1, Pallas kernels, per_device(): pl.pallas_call(functools.partial(mean_kernel, send_rows, parts), out_shap...  1.93 us
  transfers between devices with their start and end apart: 3, of which 2 were waited for; matrix products, arithmetic and copies ran while one was open for 0% of the time, Pallas kernels for 24%

profile of v3, /device:TPU:0, one launch (start us, length us, event | category | flops | bytes accessed | tf_op | source)
XLA Modules:
  0.0 47.6 jit_solution(2017943129334298556)
XLA Ops:
  0.0 2.3 %select.1 = bf16[32,48,128]{2,1,0:T(8,128)(2,1)} custom-call(bf16[1024,128]{1,0:T(8,128)(2,1)} %x_ref.1, s32[16,32]{1,0:T(8,128)} %bitcast.4, s32[1,64]{1,0:T(1,128)} %bitcast.6), custom_call_target="tpu_custom_call" | custom-call | tf_op jit(solution)/shard_map/select/pallas_call | solution.py:371
  2.3 7.3 %all-to-all-start = ((bf16[32,48,128]{2,1,0:T(8,128)(2,1)}), bf16[32,48,128]{2,1,0:T(8,128)(2,1)S(1)}, u32[]{:S(2)}, u32[]{:S(2)}) async-start(bf16[32,48,128]{2,1,0:T(8,128)(2,1)} %select.1), calls=%async_computation | async-start | bytes 786432 | tf_op jit(solution)/shard_map/all_to_all | solution.py:381
  9.6 8.3 %build.1 = (bf16[1024,1024]{1,0:T(8,128)(2,1)}, bf16[1024,1536]{1,0:T(8,128)(2,1)}, f32[1024,128]{1,0:T(8,128)}, bf16[1024,1024]{1,0:T(8,128)(2,1)S(1)}, f32[1024,128]{1,0:T(8,128)S(1)}) custom-call(s32[96]{0:T(128)} %ld.1, s32[96]{0:T(128)} %ls.1, s32[96]{0:T(128)} %rd.1, s32[96]{0:T(128)} %rs.1, s32[96]{0:T(128)} %hd.1, s32[96]{0:T(128)} %hs.1, ...), custom_call_target="tpu_custom_call" | custom-call | flops 268435456 | bytes 41943040 | tf_op jit(solution)/shard_map/build/pallas_call | solution.py:385
  17.9 4.8 %all-to-all-done._.own_ref.own_one = bf16[32,48,128]{2,1,0:T(8,128)(2,1)S(1)} async-done(((bf16[32,48,128]{2,1,0:T(8,128)(2,1)}), bf16[32,48,128]{2,1,0:T(8,128)(2,1)S(1)}, u32[]{:S(2)}, u32[]{:S(2)}) %all-to-all-start) | async-done | bytes 393248 | tf_op jit(solution)/shard_map/all_to_all | solution.py:381
  22.7 0.0 collective-permute-start
  22.8 2.1 %stage.1 = (bf16[1024,1536]{1,0:T(8,128)(2,1)S(1)}, f32[1024,128]{1,0:T(8,128)S(1)}, bf16[576,1024]{1,0:T(8,128)(2,1)S(1)}) custom-call(s32[16,32]{1,0:T(8,128)} %bitcast.5, s32[1,64]{1,0:T(1,128)} %bitcast.7, bf16[32,48,128]{2,1,0:T(8,128)(2,1)S(1)} %all-to-all-done._.own_ref.own_one, bf16[1024,1536]{1,0:T(8,128)(2,1)} %get-tuple-element.32.refs_0_, ...), custom_call_target="tpu_custom_call" | custom-call | bytes 8388608 | tf_op jit(solution)/shard_map/stage/pallas_call | solution.py:421
  24.8 0.0 collective-permute-done.other_ref.other_one
  24.8 0.0 copy-start
  24.8 0.0 copy-start.1
  24.8 0.0 copy-start.2
  24.9 0.0 copy-start.3
  24.9 0.0 copy-start.5
  24.9 1.9 %mean.1 = (bf16[1024,128]{1,0:T(8,128)(2,1)S(1)}, bf16[32,48,128]{2,1,0:T(8,128)(2,1)S(1)}) custom-call(bf16[32,48,128]{2,1,0:T(8,128)(2,1)S(1)} %all-to-all-done._.own_ref.own_one, bf16[32,48,128]{2,1,0:T(8,128)(2,1)S(1)} %collective-permute-done.other_ref.other_one, f32[1024,128]{1,0:T(8,128)S(1)} %get-tuple-element.31.agg_ref, ...), custom_call_target="tpu_custom_call" | custom-call | tf_op jit(solution)/shard_map/mean/pallas_call | solution.py:434
  26.8 0.0 copy-start.4
  26.8 15.7 %all_to_all.10.own_two = bf16[32,48,128]{2,1,0:T(8,128)(2,1)S(1)} all-to-all(bf16[32,48,128]{2,1,0:T(8,128)(2,1)S(1)} %get-tuple-element.38), channel_id=1, replica_groups=mesh['nodes'=32] {'nodes'}, dimensions={0} | all-to-all | bytes 786432 | tf_op jit(solution)/shard_map/all_to_all | solution.py:445
  42.6 0.0 collective-permute-start.1
  42.6 0.0 copy-done
  42.6 0.0 copy-done.1
  42.6 0.0 copy-done.2
  42.6 0.0 copy-done.3
  42.6 0.0 copy-done.5
  42.6 1.3 %own.1 = (f32[1024,256]{1,0:T(8,128)S(1)}, f32[1024,256]{1,0:T(8,128)S(1)}) custom-call(bf16[1024,128]{1,0:T(8,128)(2,1)S(1)} %copy-done, bf16[1024,128]{1,0:T(8,128)(2,1)S(1)} %get-tuple-element.41.mean_ref, bf16[1024,1024]{1,0:T(8,128)(2,1)S(1)} %copy-done.1, bf16[128,256]{1,0:T(8,128)(2,1)S(1)} %copy-done.2, bf16[128,256]{1,0:T(8,128)(2,1)S(1)} %copy-done.3, ...), custom_call_target="tpu_custom_call" | custom-call | flops 536870912 | bytes 8388608 | tf_op jit(solution)/shard_map/own/pallas_call | solution.py:449
  43.9 0.4 collective-permute-done.1.other_two
  44.3 0.0 copy-done.4
  44.3 3.3 %last.1 = f32[1024,256]{1,0:T(8,128)} custom-call(bf16[32,48,128]{2,1,0:T(8,128)(2,1)S(1)} %all-to-all-done._.own_ref.own_one, bf16[32,48,128]{2,1,0:T(8,128)(2,1)S(1)} %collective-permute-done.other_ref.other_one, bf16[32,48,128]{2,1,0:T(8,128)(2,1)S(1)} %all_to_all.10.own_two, bf16[32,48,128]{2,1,0:T(8,128)(2,1)S(1)} %collective-permute-done.1.other_two, ...), custom_call_target="tpu_custom_call" | custom-call | tf_op jit(solution)/shard_map/last/pallas_call | solution.py:461
Async XLA Ops:
  2.3 20.5 %all-to-all-start = ((bf16[32,48,128]{2,1,0:T(8,128)(2,1)}), bf16[32,48,128]{2,1,0:T(8,128)(2,1)S(1)}, u32[]{:S(2)}, u32[]{:S(2)}) async-start(bf16[32,48,128]{2,1,0:T(8,128)(2,1)} %select.1), calls=%async_computation | async-start | bytes 786432 | tf_op jit(solution)/shard_map/all_to_all | solution.py:381
  22.7 2.1 %collective-permute-start = (bf16[32,48,128]{2,1,0:T(8,128)(2,1)S(1)}, bf16[32,48,128]{2,1,0:T(8,128)(2,1)S(1)}, u32[]{:S(2)}, u32[]{:S(2)}) collective-permute-start(bf16[32,48,128]{2,1,0:T(8,128)(2,1)S(1)} %all-to-all-done._.own_ref.own_one), channel_id=1, source_target_pairs={{0,1},{1,0},{2,3},{3,2},{4,5},{5,4},{6,7},{7,6},{8,9},{9,8},{10,11... | collective-permute-start | bytes 1179656 | tf_op jit(solution)/shard_map/ppermute | solution.py:418
  24.8 17.7 %copy-start = (bf16[1024,128]{1,0:T(8,128)(2,1)S(1)}, bf16[1024,128]{1,0:T(8,128)(2,1)}, u32[]{:S(2)}) copy-start(bf16[1024,128]{1,0:T(8,128)(2,1)} %x_ref.1) | copy-start | bytes 786436
  24.8 17.7 %copy-start.1 = (bf16[1024,1024]{1,0:T(8,128)(2,1)S(1)}, bf16[1024,1024]{1,0:T(8,128)(2,1)}, u32[]{:S(2)}) copy-start(bf16[1024,1024]{1,0:T(8,128)(2,1)} %get-tuple-element.42.a_ref) | copy-start | bytes 6291460
  24.8 17.7 %copy-start.2 = (bf16[128,256]{1,0:T(8,128)(2,1)S(1)}, bf16[128,256]{1,0:T(8,128)(2,1)}, u32[]{:S(2)}) copy-start(bf16[128,256]{1,0:T(8,128)(2,1)} %self_one.3) | copy-start | bytes 196612
  24.9 17.7 %copy-start.3 = (bf16[128,256]{1,0:T(8,128)(2,1)S(1)}, bf16[128,256]{1,0:T(8,128)(2,1)}, u32[]{:S(2)}) copy-start(bf16[128,256]{1,0:T(8,128)(2,1)} %neigh_one.3) | copy-start | bytes 196612
  24.9 17.7 %copy-start.5 = (bf16[256,256]{1,0:T(8,128)(2,1)S(1)}, bf16[256,256]{1,0:T(8,128)(2,1)}, u32[]{:S(2)}) copy-start(bf16[256,256]{1,0:T(8,128)(2,1)} %self_two.1) | copy-start | bytes 393220
  26.8 17.5 %copy-start.4 = (bf16[256,256]{1,0:T(8,128)(2,1)S(1)}, bf16[256,256]{1,0:T(8,128)(2,1)}, u32[]{:S(2)}) copy-start(bf16[256,256]{1,0:T(8,128)(2,1)} %neigh_two.1) | copy-start | bytes 393220
  42.6 1.7 %collective-permute-start.1 = (bf16[32,48,128]{2,1,0:T(8,128)(2,1)S(1)}, bf16[32,48,128]{2,1,0:T(8,128)(2,1)S(1)}, u32[]{:S(2)}, u32[]{:S(2)}) collective-permute-start(bf16[32,48,128]{2,1,0:T(8,128)(2,1)S(1)} %all_to_all.10.own_two), channel_id=1, source_target_pairs={{0,1},{1,0},{2,3},{3,2},{4,5},{5,4},{6,7},{7,6},{8,9},{9,8},{10,11... | collective-permute-start | bytes 1179656 | tf_op jit(solution)/shard_map/ppermute | solution.py:447

commit v4 on v3

--- a/solution.py
+++ b/solution.py
@@ -71,8 +71,21 @@
     fill_send(lists_ref.shape[0], sel_ref[...], x_ref[...], send_ref)
 
 
+def halves_matrix(size, hubs):
+    half = hubs // 2
+    shape = (2 * size, 2 * size)
+    source = lax.broadcasted_iota(jnp.int32, shape, 0)
+    target = lax.broadcasted_iota(jnp.int32, shape, 1)
+    mine = lax.rem(lax.axis_index("nodes"), 2)
+    inner = lax.rem(target, size)
+    which = jnp.where(target < size, mine, 1 - mine)
+    wanted = lax.div(inner, half) * hubs + which * half + lax.rem(inner, half)
+    return jnp.where(source == wanted, 1.0, 0.0).astype(BF16)
+
+
 def build_kernel(
     cols,
+    hubs,
     parts,
     chunks,
     ld,
@@ -86,16 +99,18 @@
     rt,
     ht,
     al_hbm,
-    ar_hbm,
-    inv_hbm,
-    near_ref,
+    bound_hbm,
+    other_hbm,
+    own_ref,
+    inv_ref,
     agg_ref,
     acc,
     tiles,
     x_ref,
+    move,
     al_ref,
-    ar_ref,
-    inv_ref,
+    bound_ref,
+    other_ref,
     tile_sems,
     x_sem,
     out_sems,
@@ -103,7 +118,7 @@
     part = pl.program_id(0)
     size = acc.shape[1]
     wide = sum(cols)
-    near = wide - near_ref.shape[1] // size
+    near = cols[0] + cols[1]
     blocks = acc.shape[0] // wide
     count = lt.shape[0]
     per = count // chunks
@@ -127,6 +142,8 @@
                 moves[g][k].start()
         load_x.start()
 
+    move[...] = halves_matrix(size, hubs)
+
     def clear(i, _):
         acc[i] = jnp.zeros((size, size), F32)
         return 0
@@ -163,24 +180,25 @@
         rows = pl.ds(pl.multiple_of(b * size, size), size)
         there = pl.ds(pl.multiple_of((part * blocks + b) * size, size), size)
         return (
-            pltpu.make_async_copy(ar_ref.at[rows], ar_hbm.at[there], out_sems.at[0, b]),
-            pltpu.make_async_copy(inv_ref.at[rows], inv_hbm.at[there], out_sems.at[1, b]),
-            pltpu.make_async_copy(al_ref.at[rows], al_hbm.at[there], out_sems.at[2, b]),
+            pltpu.make_async_copy(al_ref.at[rows], al_hbm.at[there], out_sems.at[0, b]),
+            pltpu.make_async_copy(bound_ref.at[rows], bound_hbm.at[there], out_sems.at[1, b]),
+            pltpu.make_async_copy(other_ref.at[rows], other_hbm.at[there], out_sems.at[2, b]),
         )
 
     def finish(b, _):
         rows = pl.ds(pl.multiple_of(b * size, size), size)
         total = jnp.zeros((size, size), F32)
-        for c in range(wide):
+        for c in range(near):
             tile = acc[b * wide + c]
             total += tile
-            if c < cols[0]:
-                ref, at = al_ref, c
-            elif c < near:
-                ref, at = ar_ref, c - cols[0]
-            else:
-                ref, at = near_ref, c - near
+            ref, at = (al_ref, c) if c < cols[0] else (bound_ref, c - cols[0])
             ref[rows, at * size : (at + 1) * size] = tile.astype(BF16)
+        for q in range(cols[2] // 2):
+            pair = [acc[b * wide + near + 2 * q + i] for i in range(2)]
+            total += pair[0] + pair[1]
+            moved = dot(jnp.concatenate(pair, axis=1).astype(BF16), move[...]).astype(BF16)
+            own_ref[rows, q * size : (q + 1) * size] = moved[:, :size]
+            other_ref[rows, q * size : (q + 1) * size] = moved[:, size:]
         deg = 1.0 + jnp.sum(total, axis=1, keepdims=True)
         inv_ref[rows, :] = jnp.broadcast_to(1.0 / deg, (size, size))
         for copy in leave(b):
@@ -198,85 +216,123 @@
     lax.fori_loop(0, blocks, end, 0)
 
 
-def assemble(send_rows, own_ref, other_ref, dest_ref, lanes):
-    peers, per = own_ref.shape[:2]
-    half = per - send_rows
-    mine = lax.rem(lax.axis_index("nodes"), 2)
-    base = peers * send_rows
-    for o in range(peers):
-        dest_ref[o * send_rows : (o + 1) * send_rows, lanes] = own_ref[o, 0:send_rows, :]
-        for ref, h in ((own_ref, mine), (other_ref, 1 - mine)):
-            at = pl.multiple_of(base + o * 2 * half + h * half, half)
-            dest_ref[pl.ds(at, half), lanes] = ref[o, send_rows:per, :]
-
-
-def stage_kernel(lists_hbm, hub_hbm, _, *refs):
-    pairs = len(refs) // 2 - 2
-    sources, targets = refs[:pairs], refs[pairs : 2 * pairs]
-    sel_ref, lists_ref, hub_ref, sems = refs[2 * pairs :]
-    copies = fetch(((lists_hbm, lists_ref), (hub_hbm, hub_ref), *zip(sources, targets)), sems)
+def cuts_of(rows, cuts):
+    return [slice(k * rows // cuts, (k + 1) * rows // cuts) for k in range(cuts)]
+
+
+def place(first, last, got_ref, dest_ref, start, lanes=slice(None)):
+    per = last - first
+    for o in range(got_ref.shape[0]):
+        dest_ref[start + o * per : start + (o + 1) * per, lanes] = got_ref[o, first:last, :]
+
+
+def stage_kernel(
+    send_rows, parts, lists_hbm, hub_hbm, got_ref, agg_ref, own_ref, bound_in, other_in, sel_ref, sum_ref, *refs
+):
+    moved, (lists_ref, hub_ref, x_ref, sems) = refs[:-4], refs[-4:]
+    part = pl.program_id(0)
+    per = got_ref.shape[1]
+    rows, bound = bound_in.shape if parts > 1 else moved[0].shape
+    copies = fetch(((lists_hbm, lists_ref), (hub_hbm, hub_ref), *zip((bound_in, other_in), moved)), sems)
+
+    @pl.when(part == 0)
+    def _():
+        place(0, send_rows, got_ref, x_ref, 0)
+        place(send_rows, per, got_ref, x_ref, bound)
+
+    for at in cuts_of(rows, 4):
+        sum_ref[at, :] = agg_ref[at, :] + dot(own_ref[at, :], x_ref[bound:, :])
     copies[0].wait()
     copies[1].wait()
-    fill_select(lists_ref, hub_ref, sel_ref)
-    for copy in copies[2:]:
-        copy.wait()
-
-
-def far_dot(a_ref, near_ref, at, values_ref):
-    split = a_ref.shape[1]
-    return dot(a_ref[at, :], values_ref[0:split, :]) + dot(near_ref[at, :], values_ref[split:, :])
-
-
-def cuts_of(rows, cuts):
-    return [slice(k * rows // cuts, (k + 1) * rows // cuts) for k in range(cuts)]
-
-
-def mean_kernel(
-    send_rows, parts, own_ref, other_ref, agg_ref, a_ref, near_ref, inv_ref, sel_ref, mean_ref, send_ref, xr_ref
+
+    @pl.when(part == 0)
+    def _():
+        fill_select(lists_ref, hub_ref, sel_ref)
+
+    if moved:
+        copies[2].wait()
+    bound_ref = moved[0] if moved else bound_in
+    for at in cuts_of(rows, 4):
+        sum_ref[at, :] += dot(bound_ref[at, :], x_ref[0:bound, :])
+    if moved:
+        copies[3].wait()
+
+
+def mean_kernel(send_rows, parts, got_ref, sum_ref, a_ref, inv_ref, sel_ref, mean_ref, send_ref, x_ref):
+    part = pl.program_id(0)
+    rows = a_ref.shape[0]
+
+    @pl.when(part == 0)
+    def _():
+        place(send_rows, got_ref.shape[1], got_ref, x_ref, 0)
+
+    for at in cuts_of(rows, 4):
+        agg = sum_ref[at, :] + dot(a_ref[at, :], x_ref[...])
+        there = pl.ds(pl.multiple_of(part * rows + at.start, rows // 4), rows // 4)
+        mean_ref[there, :] = (agg * inv_ref[at, :]).astype(BF16)
+
+    @pl.when(part == parts - 1)
+    def _():
+        fill_send(send_rows, sel_ref[...], mean_ref[...], send_ref)
+
+
+def fill_first(both, weight, self_one, neigh_one, first):
+    width = self_one.shape[0]
+    weight[0:width, :] = self_one[...]
+    weight[width : 2 * width, :] = neigh_one[...]
+    first[...] = jnp.maximum(dot(both[...], weight[...]), 0.0).astype(BF16)
+
+
+def own_kernel(
+    send_rows,
+    x_ref,
+    mean_ref,
+    got_one,
+    got_two,
+    local_ref,
+    bound_ref,
+    own_ref,
+    self_one,
+    neigh_one,
+    self_two,
+    sum_ref,
+    part_ref,
+    both,
+    weight,
+    first,
 ):
     part = pl.program_id(0)
-    rows = a_ref.shape[0]
-
-    @pl.when(part == 0)
-    def _():
-        assemble(send_rows, own_ref, other_ref, xr_ref, slice(None))
+    rows = local_ref.shape[0]
+    nodes, width = x_ref.shape
+    near = nodes + bound_ref.shape[1]
+
+    @pl.when(part == 0)
+    def _():
+        both[0:nodes, 0:width] = x_ref[...]
+        both[0:nodes, width : 2 * width] = mean_ref[...]
+        for got_ref, lanes in ((got_one, slice(0, width)), (got_two, slice(width, 2 * width))):
+            place(0, send_rows, got_ref, both, nodes, lanes)
+            place(send_rows, got_ref.shape[1], got_ref, both, near, lanes)
+        fill_first(both, weight, self_one, neigh_one, first)
 
     for at in cuts_of(rows, 4):
-        agg = agg_ref[at, :] + far_dot(a_ref, near_ref, at, xr_ref)
-        there = pl.ds(pl.multiple_of(part * rows + at.start, rows // 4), rows // 4)
-        mean_ref[there, :] = (agg * inv_ref[at, :]).astype(BF16)
-
-    @pl.when(part == parts - 1)
-    def _():
-        fill_send(send_rows, sel_ref[...], mean_ref[...], send_ref)
-
-
-def own_kernel(x_ref, mean_ref, a_ref, self_one, neigh_one, self_two, agg_ref, part_ref, first):
-    part = pl.program_id(0)
-    rows = a_ref.shape[0]
-
-    @pl.when(part == 0)
-    def _():
-        total = dot(x_ref[...], self_one[...]) + dot(mean_ref[...], neigh_one[...])
-        first[...] = jnp.maximum(total, 0.0).astype(BF16)
-
-    for at in cuts_of(rows, 4):
-        agg_ref[at, :] = dot(a_ref[at, :], first[...])
+        sum_ref[at, :] = (
+            dot(local_ref[at, :], first[0:nodes, :])
+            + dot(bound_ref[at, :], first[nodes:near, :])
+            + dot(own_ref[at, :], first[near:, :])
+        )
     at = pl.ds(pl.multiple_of(part * rows, rows), rows)
     part_ref[...] = dot(first[at, :], self_two[...])
 
 
 def last_kernel(
     send_rows,
-    own_one,
-    other_one,
-    own_two,
-    other_two,
-    agg_ref,
+    got_one,
+    got_two,
+    sum_ref,
     part_ref,
     inv_ref,
     a_ref,
-    near_ref,
     self_one,
     neigh_one,
     neigh_two,
@@ -290,18 +346,16 @@
 ):
     part = pl.program_id(0)
     rows = a_ref.shape[0]
-    width = both.shape[1] // 2
-
-    @pl.when(part == 0)
-    def _():
-        assemble(send_rows, own_one, other_one, both, slice(0, width))
-        assemble(send_rows, own_two, other_two, both, slice(width, 2 * width))
-        weight[0:width, :] = self_one[...]
-        weight[width : 2 * width, :] = neigh_one[...]
-        first[...] = jnp.maximum(dot(both[...], weight[...]), 0.0).astype(BF16)
+    width = self_one.shape[0]
+
+    @pl.when(part == 0)
+    def _():
+        for got_ref, lanes in ((got_one, slice(0, width)), (got_two, slice(width, 2 * width))):
+            place(send_rows, got_ref.shape[1], got_ref, both, 0, lanes)
+        fill_first(both, weight, self_one, neigh_one, first)
 
     for at in cuts_of(rows, 4):
-        agg = agg_ref[at, :] + far_dot(a_ref, near_ref, at, first)
+        agg = sum_ref[at, :] + dot(a_ref[at, :], first[...])
         inv = inv_ref[at, :]
         inv = jnp.concatenate([inv] * (agg.shape[1] // inv.shape[1]), axis=1)
         mean_ref[at, :] = (agg * inv).astype(BF16)
@@ -339,7 +393,6 @@
     _, peers, send_rows = send_lists.shape
     hubs = hub_rows.shape[0]
     per = send_rows + hubs // 2
-    far = peers * (send_rows + hubs)
     cols = (nodes // size, peers * send_rows // size, peers * hubs // size)
     wide = sum(cols)
     blocks = nodes // size
@@ -381,26 +434,29 @@
     got = lax.all_to_all(send, "nodes", split_axis=0, concat_axis=0, tiled=True)
 
     chunks = 2
-    near = nodes
-    a_local, a_far, inv, a_near, agg = pl.pallas_call(
-        functools.partial(build_kernel, cols, parts, chunks),
+    bound = peers * send_rows
+    other_rows = peers * (hubs // 2)
+    a_local, a_bound, a_other, a_own, inv, agg = pl.pallas_call(
+        functools.partial(build_kernel, cols, hubs, parts, chunks),
         out_shape=(
             pltpu.HBM((nodes, nodes), BF16),
-            pltpu.HBM((nodes, far - near), BF16),
-            pltpu.HBM((nodes, size), F32),
-            kept((nodes, near), BF16),
+            pltpu.HBM((nodes, bound), BF16),
+            pltpu.HBM((nodes, other_rows), BF16),
+            kept((nodes, other_rows), BF16),
+            kept((nodes, size), F32),
             kept((nodes, f_in), F32),
         ),
         grid=(parts,),
         in_specs=[whole(pltpu.SMEM)] * 6 + [hbm] * 4,
-        out_specs=(hbm, hbm, hbm, split(near), split(f_in)),
+        out_specs=(hbm, hbm, hbm, split(other_rows), split(size), split(f_in)),
         scratch_shapes=[
             pltpu.VMEM((blocks // parts * wide + spare, size, size), F32),
             pltpu.VMEM((3, tiles, size, size), BF16),
             pltpu.VMEM((nodes, f_in), BF16),
+            pltpu.VMEM((2 * size, 2 * size), BF16),
             pltpu.VMEM((rows, nodes), BF16),
-            pltpu.VMEM((rows, far - near), BF16),
-            pltpu.VMEM((rows, size), F32),
+            pltpu.VMEM((rows, bound), BF16),
+            pltpu.VMEM((rows, other_rows), BF16),
             dma((3, chunks)),
             dma(()),
             dma((3, blocks // parts)),
@@ -412,69 +468,81 @@
         *in_hbm(local_dst, local_src, remote_dst, remote_src, hub_dst, hub_src),
         *in_hbm(features, local_tiles, remote_tiles, hub_tiles),
     )
-    built = (got, a_local, a_far, inv, a_near, agg)
-    got, a_local, a_far, inv, a_near, agg = lax.optimization_barrier(built)
+    built = (got, a_local, a_bound, a_other, a_own, inv, agg)
+    got, a_local, a_bound, a_other, a_own, inv, agg = lax.optimization_barrier(built)
 
     other = lax.ppermute(got, "nodes", swap)
 
-    staged = (a_far, inv) if parts == 1 else ()
-    *moved, sel = pl.pallas_call(
-        stage_kernel,
-        out_shape=(*(kept(x.shape, x.dtype) for x in staged), kept((chosen, nodes), BF16)),
-        in_specs=[hbm, hbm, whole(pl.ANY)] + [hbm] * len(staged),
-        out_specs=(vm,) * (1 + len(staged)),
-        scratch_shapes=[*tables, dma((2 + len(staged),))],
-        compiler_params=params(8 if parts == 1 else 16),
+    far = (a_bound, a_other)
+    moved = far if parts == 1 else ()
+    sel, agg, *moved = pl.pallas_call(
+        functools.partial(stage_kernel, send_rows, parts),
+        out_shape=(
+            kept((chosen, nodes), BF16),
+            kept((nodes, f_in), F32),
+            *(kept(x.shape, x.dtype) for x in moved),
+        ),
+        grid=(parts,),
+        in_specs=[hbm, hbm, vm, split(f_in), split(other_rows)]
+        + ([hbm, hbm] if moved else [split(bound), whole(pl.ANY)]),
+        out_specs=(vm, split(f_in), *([vm] * len(moved))),
+        scratch_shapes=[*tables, pltpu.VMEM((bound + other_rows, f_in), BF16), dma((2 + len(moved),))],
+        compiler_params=params(12 if parts == 1 else 32),
         cost_estimate=pl.CostEstimate(flops=0, bytes_accessed=8 * MIB, transcendentals=0),
         name="stage",
-    )(*in_hbm(lists, hub_row), got, *in_hbm(*staged))
-    if staged:
-        a_far, inv = moved
+    )(*in_hbm(lists, hub_row), got, agg, a_own, *(in_hbm(*far) if moved else far))
+    if moved:
+        a_bound, a_other = moved
 
     mean, send = pl.pallas_call(
         functools.partial(mean_kernel, send_rows, parts),
         out_shape=(sds((nodes, f_in), BF16), sds(send.shape, BF16)),
         grid=(parts,),
-        in_specs=[vm] * 2 + [split(f_in), split(far - near), split(near), split(size), vm],
+        in_specs=[vm, split(f_in), split(other_rows), split(size), vm],
         out_specs=(vm, vm),
-        scratch_shapes=[pltpu.VMEM((far, f_in), BF16)],
+        scratch_shapes=[pltpu.VMEM((other_rows, f_in), BF16)],
         compiler_params=params(8 if parts == 1 else 48),
         name="mean",
-    )(got, other, agg, a_far, a_near, inv, sel)
+    )(other, agg, a_other, inv, sel)
 
     got_two = lax.all_to_all(send, "nodes", split_axis=0, concat_axis=0, tiled=True)
     got_two, mean = lax.optimization_barrier((got_two, mean))
     other_two = lax.ppermute(got_two, "nodes", swap)
 
+    near = nodes + bound + other_rows
     agg, part = pl.pallas_call(
-        own_kernel,
+        functools.partial(own_kernel, send_rows),
         out_shape=(sds((nodes, hid), F32), sds((nodes, hid), F32)),
         grid=(parts,),
-        in_specs=[vm, vm, split(nodes), vm, vm, vm],
+        in_specs=[vm] * 4 + [split(nodes), split(bound), split(other_rows)] + [vm] * 3,
         out_specs=(split(hid), split(hid)),
-        scratch_shapes=[pltpu.VMEM((nodes, hid), BF16)],
-        compiler_params=params(16),
-        cost_estimate=pl.CostEstimate(flops=2 * nodes * nodes * hid, bytes_accessed=8 * MIB, transcendentals=0),
+        scratch_shapes=[
+            pltpu.VMEM((near, 2 * f_in), BF16),
+            pltpu.VMEM((2 * f_in, hid), BF16),
+            pltpu.VMEM((near, hid), BF16),
+        ],
+        compiler_params=params(16 if parts == 1 else 48),
+        cost_estimate=pl.CostEstimate(flops=2 * nodes * near * hid, bytes_accessed=8 * MIB, transcendentals=0),
         name="own",
-    )(features, mean, a_local, self_one, neigh_one, self_two)
+    )(features, mean, got, got_two, a_local, a_bound, a_own, self_one, neigh_one, self_two)
 
     return pl.pallas_call(
         functools.partial(last_kernel, send_rows),
         out_shape=sds((nodes, hid), F32),
         grid=(parts,),
-        in_specs=[vm] * 4 + [split(hid), split(hid), split(size), split(far - near), split(near)] + [vm] * 3,
+        in_specs=[vm] * 2 + [split(hid), split(hid), split(size), split(other_rows)] + [vm] * 3,
         out_specs=hbm,
         scratch_shapes=[
-            pltpu.VMEM((far, 2 * f_in), BF16),
+            pltpu.VMEM((other_rows, 2 * f_in), BF16),
             pltpu.VMEM((2 * f_in, hid), BF16),
-            pltpu.VMEM((far, hid), BF16),
+            pltpu.VMEM((other_rows, hid), BF16),
             pltpu.VMEM((rows, hid), BF16),
             pltpu.VMEM((rows, hid), F32),
             dma((4,)),
         ],
         compiler_params=params(16 if parts == 1 else 56),
         name="last",
-    )(got, other, got_two, other_two, agg, part, inv, a_far, a_near, self_one, neigh_one, neigh_two)
+    )(other, other_two, agg, part, inv, a_other, self_one, neigh_one, neigh_two)
 
 
 def solution(mesh):

time: 48 us -> 46.9 us (0.977)
  waiting for transfers between devices: 5.25 us -> 4.28 us
    pallas_call x3, Pallas kernels: 11.7 us -> 13.8 us  [the longest x1 8.9 us: per_device(): pl.pallas_call(functools.partial(build_kernel, cols, hubs, parts, chunks)...]
    pallas_call x1, Pallas kernels: 3.29 us -> 1.95 us  [per_device(): pl.pallas_call(functools.partial(last_kernel, send_rows), out_shape=sds((...]
    pallas_call x1, Pallas kernels: 1.93 us -> 1.06 us  [per_device(): pl.pallas_call(functools.partial(mean_kernel, send_rows, parts), out_shap...]
    all_to_all x1, waiting for transfers between devices: 4.84 us -> 4.27 us  [per_device(): got = lax.all_to_all(send, 'nodes', split_axis=0, concat_axis=0, tiled=True)]
  transfers between devices with their start and end apart: 3 -> 3, of which waited for: 2 -> 1; matrix products, arithmetic and copies ran while one was open for 0% -> 0% of each run, Pallas kernels for 24% -> 30%
where the time goes in v4:
time: 46.9 us; the launch traced here: 46.5 us
  Pallas kernels  19 us (41%)
  blocking collectives  15.7 us (33%)
  starting transfers between devices  7.31 us (16%)
  waiting for transfers between devices  4.28 us (9%)
    all_to_all x1, blocking collectives, per_device(): lax.all_to_all(send, 'nodes', split_axis=0, concat_axis=0, tiled=True)  15.7 us
    pallas_call x1, Pallas kernels, per_device(): pl.pallas_call(functools.partial(build_kernel, cols, hubs, parts, chunks)...  8.9 us
    all_to_all x1, starting transfers between devices, per_device(): got = lax.all_to_all(send, 'nodes', split_axis=0, concat_axis=0, tiled=True)  7.3 us
    all_to_all x1, waiting for transfers between devices, per_device(): got = lax.all_to_all(send, 'nodes', split_axis=0, concat_axis=0, tiled=True)  4.27 us
    pallas_call x1, Pallas kernels, per_device(): pl.pallas_call(functools.partial(stage_kernel, send_rows, parts), out_sha...  2.57 us
    pallas_call x1, Pallas kernels, per_device(): pl.pallas_call(functools.partial(own_kernel, send_rows), out_shape=(sds((...  2.3 us
    pallas_call x1, Pallas kernels, per_device(): pl.pallas_call(select_kernel, out_shape=kept((peers, per, f_in), BF16), i...  2.25 us
    pallas_call x1, Pallas kernels, per_device(): pl.pallas_call(functools.partial(last_kernel, send_rows), out_shape=sds((...  1.95 us
  transfers between devices with their start and end apart: 3, of which 1 were waited for; matrix products, arithmetic and copies ran while one was open for 0% of the time, Pallas kernels for 30%

profile of v4, /device:TPU:0, one launch (start us, length us, event | category | flops | bytes accessed | tf_op | source)
XLA Modules:
  0.0 46.5 jit_solution(14902243886830270893)
XLA Ops:
  0.0 2.3 %select.1 = bf16[32,48,128]{2,1,0:T(8,128)(2,1)} custom-call(bf16[1024,128]{1,0:T(8,128)(2,1)} %x_ref.1, s32[16,32]{1,0:T(8,128)} %bitcast.4, s32[1,64]{1,0:T(1,128)} %bitcast.6), custom_call_target="tpu_custom_call" | custom-call | tf_op jit(solution)/shard_map/select/pallas_call | solution.py:424
  2.3 7.3 %all-to-all-start = ((bf16[32,48,128]{2,1,0:T(8,128)(2,1)}), bf16[32,48,128]{2,1,0:T(8,128)(2,1)S(1)}, u32[]{:S(2)}, u32[]{:S(2)}) async-start(bf16[32,48,128]{2,1,0:T(8,128)(2,1)} %select.1), calls=%async_computation | async-start | bytes 786432 | tf_op jit(solution)/shard_map/all_to_all | solution.py:434
  9.6 8.9 %build.1 = (bf16[1024,1024]{1,0:T(8,128)(2,1)}, bf16[1024,512]{1,0:T(8,128)(2,1)}, bf16[1024,1024]{1,0:T(8,128)(2,1)}, bf16[1024,1024]{1,0:T(8,128)(2,1)S(1)}, f...) custom-call(s32[96]{0:T(128)} %ld.1, s32[96]{0:T(128)} %ls.1, s32[96]{0:T(128)} %rd.1, s32[96]{0:T(128)} %rs.1, s32[96]{0:T(128)} %hd.1, ...), custom_call_target="tpu_custom_call" | custom-call | flops 268435456 | bytes 41943040 | tf_op jit(solution)/shard_map/build/pallas_call | solution.py:439
  18.5 4.3 %all-to-all-done.got_ref.got_one = bf16[32,48,128]{2,1,0:T(8,128)(2,1)S(1)} async-done(((bf16[32,48,128]{2,1,0:T(8,128)(2,1)}), bf16[32,48,128]{2,1,0:T(8,128)(2,1)S(1)}, u32[]{:S(2)}, u32[]{:S(2)}) %all-to-all-start) | async-done | bytes 393248 | tf_op jit(solution)/shard_map/all_to_all | solution.py:434
  22.7 0.0 collective-permute-start
  22.8 2.6 %stage.1 = (bf16[576,1024]{1,0:T(8,128)(2,1)S(1)}, f32[1024,128]{1,0:T(8,128)S(1)}, bf16[1024,512]{1,0:T(8,128)(2,1)S(1)}, bf16[1024,1024]{1,0:T(8,128)(2,1)S(1)}) custom-call(s32[16,32]{1,0:T(8,128)} %bitcast.5, s32[1,64]{1,0:T(1,128)} %bitcast.7, bf16[32,48,128]{2,1,0:T(8,128)(2,1)S(1)} %all-to-all-done.got_ref.got_one, ...), custom_call_target="tpu_custom_call" | custom-call | bytes 8388608 | tf_op jit(solution)/shard_map/stage/pallas_call | solution.py:478
  25.3 0.0 collective-permute-done.got_ref.got_one
  25.3 0.0 copy-start
  25.4 0.0 copy-start.1
  25.4 0.0 copy-start.2
  25.4 0.0 copy-start.3
  25.4 0.0 copy-start.4
  25.4 1.1 %mean.1 = (bf16[1024,128]{1,0:T(8,128)(2,1)S(1)}, bf16[32,48,128]{2,1,0:T(8,128)(2,1)S(1)}) custom-call(bf16[32,48,128]{2,1,0:T(8,128)(2,1)S(1)} %collective-permute-done.got_ref.got_one, f32[1024,128]{1,0:T(8,128)S(1)} %get-tuple-element.39.sum_ref, bf16[1024,1024]{1,0:T(8,128)(2,1)S(1)} %get-tuple-element.40.a_ref, ...), custom_call_target="tpu_custom_call" | custom-call | tf_op jit(solution)/shard_map/mean/pallas_call | solution.py:497
  26.5 15.7 %all_to_all.10.got_two = bf16[32,48,128]{2,1,0:T(8,128)(2,1)S(1)} all-to-all(bf16[32,48,128]{2,1,0:T(8,128)(2,1)S(1)} %get-tuple-element.43), channel_id=1, replica_groups=mesh['nodes'=32] {'nodes'}, dimensions={0} | all-to-all | bytes 786432 | tf_op jit(solution)/shard_map/all_to_all | solution.py:508
  42.2 0.0 collective-permute-start.1
  42.2 0.0 copy-done
  42.2 0.0 copy-done.1
  42.2 0.0 copy-done.2
  42.2 0.0 copy-done.3
  42.2 0.0 copy-done.4
  42.2 0.0 copy-start.5
  42.2 2.3 %own.1 = (f32[1024,256]{1,0:T(8,128)S(1)}, f32[1024,256]{1,0:T(8,128)S(1)}) custom-call(bf16[1024,128]{1,0:T(8,128)(2,1)S(1)} %copy-done, bf16[1024,128]{1,0:T(8,128)(2,1)S(1)} %get-tuple-element.46.mean_ref, bf16[32,48,128]{2,1,0:T(8,128)(2,1)S(1)} %all-to-all-done.got_ref.got_one, bf16[32,48,128]{2,1,0:T(8,128)(2,1)S(1)} %all_to_all.10.got_two, ...), custom_call_target="tpu_custom_call" | custom-call | flops 1342177280 | bytes 8388608 | tf_op jit(solution)/shard_map/own/pallas_call | solution.py:513
  44.6 0.0 collective-permute-done.1.got_two
  44.6 0.0 copy-done.5
  44.6 1.9 %last.1 = f32[1024,256]{1,0:T(8,128)} custom-call(bf16[32,48,128]{2,1,0:T(8,128)(2,1)S(1)} %collective-permute-done.got_ref.got_one, bf16[32,48,128]{2,1,0:T(8,128)(2,1)S(1)} %collective-permute-done.1.got_two, f32[1024,256]{1,0:T(8,128)S(1)} %get-tuple-element.49.sum_ref, f32[1024,256]{1,0:T(8,128)S(1)} %get-tuple-element.50.part_ref, ...), custom_call_target="tpu_custom_call" | custom-call | tf_op jit(solution)/shard_map/last/pallas_call | solution.py:529
Async XLA Ops:
  2.3 20.5 %all-to-all-start = ((bf16[32,48,128]{2,1,0:T(8,128)(2,1)}), bf16[32,48,128]{2,1,0:T(8,128)(2,1)S(1)}, u32[]{:S(2)}, u32[]{:S(2)}) async-start(bf16[32,48,128]{2,1,0:T(8,128)(2,1)} %select.1), calls=%async_computation | async-start | bytes 786432 | tf_op jit(solution)/shard_map/all_to_all | solution.py:434
  22.7 2.6 %collective-permute-start = (bf16[32,48,128]{2,1,0:T(8,128)(2,1)S(1)}, bf16[32,48,128]{2,1,0:T(8,128)(2,1)S(1)}, u32[]{:S(2)}, u32[]{:S(2)}) collective-permute-start(bf16[32,48,128]{2,1,0:T(8,128)(2,1)S(1)} %all-to-all-done.got_ref.got_one), channel_id=1, source_target_pairs={{0,1},{1,0},{2,3},{3,2},{4,5},{5,4},{6,7},{7,6},{8,9},{9,8},{10,11... | collective-permute-start | bytes 1179656 | tf_op jit(solution)/shard_map/ppermute | solution.py:474
  25.3 16.9 %copy-start = (bf16[1024,128]{1,0:T(8,128)(2,1)S(1)}, bf16[1024,128]{1,0:T(8,128)(2,1)}, u32[]{:S(2)}) copy-start(bf16[1024,128]{1,0:T(8,128)(2,1)} %x_ref.1) | copy-start | bytes 786436
  25.4 16.9 %copy-start.1 = (bf16[1024,1024]{1,0:T(8,128)(2,1)S(1)}, bf16[1024,1024]{1,0:T(8,128)(2,1)}, u32[]{:S(2)}) copy-start(bf16[1024,1024]{1,0:T(8,128)(2,1)} %get-tuple-element.47.local_ref) | copy-start | bytes 6291460
  25.4 16.9 %copy-start.2 = (bf16[128,256]{1,0:T(8,128)(2,1)S(1)}, bf16[128,256]{1,0:T(8,128)(2,1)}, u32[]{:S(2)}) copy-start(bf16[128,256]{1,0:T(8,128)(2,1)} %self_one.3) | copy-start | bytes 196612
  25.4 16.8 %copy-start.3 = (bf16[128,256]{1,0:T(8,128)(2,1)S(1)}, bf16[128,256]{1,0:T(8,128)(2,1)}, u32[]{:S(2)}) copy-start(bf16[128,256]{1,0:T(8,128)(2,1)} %neigh_one.3) | copy-start | bytes 196612
  25.4 16.8 %copy-start.4 = (bf16[256,256]{1,0:T(8,128)(2,1)S(1)}, bf16[256,256]{1,0:T(8,128)(2,1)}, u32[]{:S(2)}) copy-start(bf16[256,256]{1,0:T(8,128)(2,1)} %self_two.1) | copy-start | bytes 393220
  42.2 2.4 %collective-permute-start.1 = (bf16[32,48,128]{2,1,0:T(8,128)(2,1)S(1)}, bf16[32,48,128]{2,1,0:T(8,128)(2,1)S(1)}, u32[]{:S(2)}, u32[]{:S(2)}) collective-permute-start(bf16[32,48,128]{2,1,0:T(8,128)(2,1)S(1)} %all_to_all.10.got_two), channel_id=1, source_target_pairs={{0,1},{1,0},{2,3},{3,2},{4,5},{5,4},{6,7},{7,6},{8,9},{9,8},{10,11... | collective-permute-start | bytes 1179656 | tf_op jit(solution)/shard_map/ppermute | solution.py:510
  42.2 2.3 %copy-start.5 = (bf16[256,256]{1,0:T(8,128)(2,1)S(1)}, bf16[256,256]{1,0:T(8,128)(2,1)}, u32[]{:S(2)}) copy-start(bf16[256,256]{1,0:T(8,128)(2,1)} %neigh_two.1) | copy-start | bytes 393220

commit v5 on v4

--- a/solution.py
+++ b/solution.py
@@ -240,8 +240,6 @@
         place(0, send_rows, got_ref, x_ref, 0)
         place(send_rows, per, got_ref, x_ref, bound)
 
-    for at in cuts_of(rows, 4):
-        sum_ref[at, :] = agg_ref[at, :] + dot(own_ref[at, :], x_ref[bound:, :])
     copies[0].wait()
     copies[1].wait()
 
@@ -253,7 +251,8 @@
         copies[2].wait()
     bound_ref = moved[0] if moved else bound_in
     for at in cuts_of(rows, 4):
-        sum_ref[at, :] += dot(bound_ref[at, :], x_ref[0:bound, :])
+        total = dot(own_ref[at, :], x_ref[bound:, :]) + dot(bound_ref[at, :], x_ref[0:bound, :])
+        sum_ref[at, :] = agg_ref[at, :] + total
     if moved:
         copies[3].wait()
 
@@ -354,17 +353,23 @@
             place(send_rows, got_ref.shape[1], got_ref, both, 0, lanes)
         fill_first(both, weight, self_one, neigh_one, first)
 
-    for at in cuts_of(rows, 4):
+    outs = []
+
+    def leave(k, at):
+        out_ref[at, :] = jnp.maximum(part_ref[at, :] + dot(mean_ref[at, :], neigh_two[...]), 0.0)
+        there = pl.ds(pl.multiple_of(part * rows + at.start, rows // 4), rows // 4)
+        outs.append(pltpu.make_async_copy(out_ref.at[at], out_hbm.at[there], sems.at[k]))
+        outs[k].start()
+
+    cuts = cuts_of(rows, 4)
+    for k, at in enumerate(cuts):
         agg = sum_ref[at, :] + dot(a_ref[at, :], first[...])
         inv = inv_ref[at, :]
         inv = jnp.concatenate([inv] * (agg.shape[1] // inv.shape[1]), axis=1)
         mean_ref[at, :] = (agg * inv).astype(BF16)
-    outs = []
-    for k, at in enumerate(cuts_of(rows, 4)):
-        out_ref[at, :] = jnp.maximum(part_ref[at, :] + dot(mean_ref[at, :], neigh_two[...]), 0.0)
-        there = pl.ds(pl.multiple_of(part * rows + at.start, rows // 4), rows // 4)
-        outs.append(pltpu.make_async_copy(out_ref.at[at], out_hbm.at[there], sems.at[k]))
-        outs[k].start()
+        if k:
+            leave(k - 1, cuts[k - 1])
+    leave(3, cuts[3])
     for copy in outs:
         copy.wait()
 

time: 46.9 us -> 46.7 us (level)
  transfers between devices with their start and end apart: 3 -> 3, of which waited for: 1 -> 1; matrix products, arithmetic and copies ran while one was open for 0% -> 0% of each run, Pallas kernels for 30% -> 29%
where the time goes in v5:
time: 46.7 us; the launch traced here: 46.3 us
  Pallas kernels  18.8 us (40%)
  blocking collectives  15.7 us (34%)
  starting transfers between devices  7.31 us (16%)
  waiting for transfers between devices  4.28 us (9%)
    all_to_all x1, blocking collectives, per_device(): lax.all_to_all(send, 'nodes', split_axis=0, concat_axis=0, tiled=True)  15.7 us
    pallas_call x1, Pallas kernels, per_device(): pl.pallas_call(functools.partial(build_kernel, cols, hubs, parts, chunks)...  8.9 us
    all_to_all x1, starting transfers between devices, per_device(): got = lax.all_to_all(send, 'nodes', split_axis=0, concat_axis=0, tiled=True)  7.3 us
    all_to_all x1, waiting for transfers between devices, per_device(): got = lax.all_to_all(send, 'nodes', split_axis=0, concat_axis=0, tiled=True)  4.27 us
    pallas_call x1, Pallas kernels, per_device(): pl.pallas_call(functools.partial(own_kernel, send_rows), out_shape=(sds((...  2.3 us
    pallas_call x1, Pallas kernels, per_device(): pl.pallas_call(functools.partial(stage_kernel, send_rows, parts), out_sha...  2.26 us
    pallas_call x1, Pallas kernels, per_device(): pl.pallas_call(select_kernel, out_shape=kept((peers, per, f_in), BF16), i...  2.25 us
    pallas_call x1, Pallas kernels, per_device(): pl.pallas_call(functools.partial(last_kernel, send_rows), out_shape=sds((...  1.99 us
  transfers between devices with their start and end apart: 3, of which 1 were waited for; matrix products, arithmetic and copies ran while one was open for 0% of the time, Pallas kernels for 29%

profile of v5, /device:TPU:0, one launch (start us, length us, event | category | flops | bytes accessed | tf_op | source)
XLA Modules:
  0.0 46.3 jit_solution(4031677831761827300)
XLA Ops:
  0.0 2.3 %select.1 = bf16[32,48,128]{2,1,0:T(8,128)(2,1)} custom-call(bf16[1024,128]{1,0:T(8,128)(2,1)} %x_ref.1, s32[16,32]{1,0:T(8,128)} %bitcast.4, s32[1,64]{1,0:T(1,128)} %bitcast.6), custom_call_target="tpu_custom_call" | custom-call | tf_op jit(solution)/shard_map/select/pallas_call | solution.py:429
  2.3 7.3 %all-to-all-start = ((bf16[32,48,128]{2,1,0:T(8,128)(2,1)}), bf16[32,48,128]{2,1,0:T(8,128)(2,1)S(1)}, u32[]{:S(2)}, u32[]{:S(2)}) async-start(bf16[32,48,128]{2,1,0:T(8,128)(2,1)} %select.1), calls=%async_computation | async-start | bytes 786432 | tf_op jit(solution)/shard_map/all_to_all | solution.py:439
  9.6 8.9 %build.1 = (bf16[1024,1024]{1,0:T(8,128)(2,1)}, bf16[1024,512]{1,0:T(8,128)(2,1)}, bf16[1024,1024]{1,0:T(8,128)(2,1)}, bf16[1024,1024]{1,0:T(8,128)(2,1)S(1)}, f...) custom-call(s32[96]{0:T(128)} %ld.1, s32[96]{0:T(128)} %ls.1, s32[96]{0:T(128)} %rd.1, s32[96]{0:T(128)} %rs.1, s32[96]{0:T(128)} %hd.1, ...), custom_call_target="tpu_custom_call" | custom-call | flops 268435456 | bytes 41943040 | tf_op jit(solution)/shard_map/build/pallas_call | solution.py:444
  18.5 4.3 %all-to-all-done.got_ref.got_one = bf16[32,48,128]{2,1,0:T(8,128)(2,1)S(1)} async-done(((bf16[32,48,128]{2,1,0:T(8,128)(2,1)}), bf16[32,48,128]{2,1,0:T(8,128)(2,1)S(1)}, u32[]{:S(2)}, u32[]{:S(2)}) %all-to-all-start) | async-done | bytes 393248 | tf_op jit(solution)/shard_map/all_to_all | solution.py:439
  22.7 0.0 collective-permute-start
  22.8 2.3 %stage.1 = (bf16[576,1024]{1,0:T(8,128)(2,1)S(1)}, f32[1024,128]{1,0:T(8,128)S(1)}, bf16[1024,512]{1,0:T(8,128)(2,1)S(1)}, bf16[1024,1024]{1,0:T(8,128)(2,1)S(1)}) custom-call(s32[16,32]{1,0:T(8,128)} %bitcast.5, s32[1,64]{1,0:T(1,128)} %bitcast.7, bf16[32,48,128]{2,1,0:T(8,128)(2,1)S(1)} %all-to-all-done.got_ref.got_one, ...), custom_call_target="tpu_custom_call" | custom-call | bytes 8388608 | tf_op jit(solution)/shard_map/stage/pallas_call | solution.py:483
  25.0 0.0 collective-permute-done.got_ref.got_one
  25.0 0.0 copy-start
  25.0 0.0 copy-start.1
  25.1 0.0 copy-start.2
  25.1 0.0 copy-start.3
  25.1 0.0 copy-start.4
  25.1 1.1 %mean.1 = (bf16[1024,128]{1,0:T(8,128)(2,1)S(1)}, bf16[32,48,128]{2,1,0:T(8,128)(2,1)S(1)}) custom-call(bf16[32,48,128]{2,1,0:T(8,128)(2,1)S(1)} %collective-permute-done.got_ref.got_one, f32[1024,128]{1,0:T(8,128)S(1)} %get-tuple-element.39.sum_ref, bf16[1024,1024]{1,0:T(8,128)(2,1)S(1)} %get-tuple-element.40.a_ref, ...), custom_call_target="tpu_custom_call" | custom-call | tf_op jit(solution)/shard_map/mean/pallas_call | solution.py:502
  26.2 15.7 %all_to_all.10.got_two = bf16[32,48,128]{2,1,0:T(8,128)(2,1)S(1)} all-to-all(bf16[32,48,128]{2,1,0:T(8,128)(2,1)S(1)} %get-tuple-element.43), channel_id=1, replica_groups=mesh['nodes'=32] {'nodes'}, dimensions={0} | all-to-all | bytes 786432 | tf_op jit(solution)/shard_map/all_to_all | solution.py:513
  41.9 0.0 collective-permute-start.1
  41.9 0.0 copy-done
  41.9 0.0 copy-done.1
  41.9 0.0 copy-done.2
  41.9 0.0 copy-done.3
  41.9 0.0 copy-done.4
  41.9 0.0 copy-start.5
  41.9 2.3 %own.1 = (f32[1024,256]{1,0:T(8,128)S(1)}, f32[1024,256]{1,0:T(8,128)S(1)}) custom-call(bf16[1024,128]{1,0:T(8,128)(2,1)S(1)} %copy-done, bf16[1024,128]{1,0:T(8,128)(2,1)S(1)} %get-tuple-element.46.mean_ref, bf16[32,48,128]{2,1,0:T(8,128)(2,1)S(1)} %all-to-all-done.got_ref.got_one, bf16[32,48,128]{2,1,0:T(8,128)(2,1)S(1)} %all_to_all.10.got_two, ...), custom_call_target="tpu_custom_call" | custom-call | flops 1342177280 | bytes 8388608 | tf_op jit(solution)/shard_map/own/pallas_call | solution.py:518
  44.3 0.0 collective-permute-done.1.got_two
  44.3 0.0 copy-done.5
  44.3 2.0 %last.1 = f32[1024,256]{1,0:T(8,128)} custom-call(bf16[32,48,128]{2,1,0:T(8,128)(2,1)S(1)} %collective-permute-done.got_ref.got_one, bf16[32,48,128]{2,1,0:T(8,128)(2,1)S(1)} %collective-permute-done.1.got_two, f32[1024,256]{1,0:T(8,128)S(1)} %get-tuple-element.49.sum_ref, f32[1024,256]{1,0:T(8,128)S(1)} %get-tuple-element.50.part_ref, ...), custom_call_target="tpu_custom_call" | custom-call | tf_op jit(solution)/shard_map/last/pallas_call | solution.py:534
Async XLA Ops:
  2.3 20.5 %all-to-all-start = ((bf16[32,48,128]{2,1,0:T(8,128)(2,1)}), bf16[32,48,128]{2,1,0:T(8,128)(2,1)S(1)}, u32[]{:S(2)}, u32[]{:S(2)}) async-start(bf16[32,48,128]{2,1,0:T(8,128)(2,1)} %select.1), calls=%async_computation | async-start | bytes 786432 | tf_op jit(solution)/shard_map/all_to_all | solution.py:439
  22.7 2.3 %collective-permute-start = (bf16[32,48,128]{2,1,0:T(8,128)(2,1)S(1)}, bf16[32,48,128]{2,1,0:T(8,128)(2,1)S(1)}, u32[]{:S(2)}, u32[]{:S(2)}) collective-permute-start(bf16[32,48,128]{2,1,0:T(8,128)(2,1)S(1)} %all-to-all-done.got_ref.got_one), channel_id=1, source_target_pairs={{0,1},{1,0},{2,3},{3,2},{4,5},{5,4},{6,7},{7,6},{8,9},{9,8},{10,11... | collective-permute-start | bytes 1179656 | tf_op jit(solution)/shard_map/ppermute | solution.py:479
  25.0 16.9 %copy-start = (bf16[1024,128]{1,0:T(8,128)(2,1)S(1)}, bf16[1024,128]{1,0:T(8,128)(2,1)}, u32[]{:S(2)}) copy-start(bf16[1024,128]{1,0:T(8,128)(2,1)} %x_ref.1) | copy-start | bytes 786436
  25.0 16.9 %copy-start.1 = (bf16[1024,1024]{1,0:T(8,128)(2,1)S(1)}, bf16[1024,1024]{1,0:T(8,128)(2,1)}, u32[]{:S(2)}) copy-start(bf16[1024,1024]{1,0:T(8,128)(2,1)} %get-tuple-element.47.local_ref) | copy-start | bytes 6291460
  25.1 16.9 %copy-start.2 = (bf16[128,256]{1,0:T(8,128)(2,1)S(1)}, bf16[128,256]{1,0:T(8,128)(2,1)}, u32[]{:S(2)}) copy-start(bf16[128,256]{1,0:T(8,128)(2,1)} %self_one.3) | copy-start | bytes 196612
  25.1 16.8 %copy-start.3 = (bf16[128,256]{1,0:T(8,128)(2,1)S(1)}, bf16[128,256]{1,0:T(8,128)(2,1)}, u32[]{:S(2)}) copy-start(bf16[128,256]{1,0:T(8,128)(2,1)} %neigh_one.3) | copy-start | bytes 196612
  25.1 16.8 %copy-start.4 = (bf16[256,256]{1,0:T(8,128)(2,1)S(1)}, bf16[256,256]{1,0:T(8,128)(2,1)}, u32[]{:S(2)}) copy-start(bf16[256,256]{1,0:T(8,128)(2,1)} %self_two.1) | copy-start | bytes 393220
  41.9 2.4 %collective-permute-start.1 = (bf16[32,48,128]{2,1,0:T(8,128)(2,1)S(1)}, bf16[32,48,128]{2,1,0:T(8,128)(2,1)S(1)}, u32[]{:S(2)}, u32[]{:S(2)}) collective-permute-start(bf16[32,48,128]{2,1,0:T(8,128)(2,1)S(1)} %all_to_all.10.got_two), channel_id=1, source_target_pairs={{0,1},{1,0},{2,3},{3,2},{4,5},{5,4},{6,7},{7,6},{8,9},{9,8},{10,11... | collective-permute-start | bytes 1179656 | tf_op jit(solution)/shard_map/ppermute | solution.py:515
  41.9 2.3 %copy-start.5 = (bf16[256,256]{1,0:T(8,128)(2,1)S(1)}, bf16[256,256]{1,0:T(8,128)(2,1)}, u32[]{:S(2)}) copy-start(bf16[256,256]{1,0:T(8,128)(2,1)} %neigh_two.1) | copy-start | bytes 393220

commit v6 on v5

--- a/solution.py
+++ b/solution.py
@@ -101,8 +101,9 @@
     al_hbm,
     bound_hbm,
     other_hbm,
+    inv_hbm,
+    kept_ref,
     own_ref,
-    inv_ref,
     agg_ref,
     acc,
     tiles,
@@ -111,6 +112,7 @@
     al_ref,
     bound_ref,
     other_ref,
+    inv_ref,
     tile_sems,
     x_sem,
     out_sems,
@@ -183,6 +185,7 @@
             pltpu.make_async_copy(al_ref.at[rows], al_hbm.at[there], out_sems.at[0, b]),
             pltpu.make_async_copy(bound_ref.at[rows], bound_hbm.at[there], out_sems.at[1, b]),
             pltpu.make_async_copy(other_ref.at[rows], other_hbm.at[there], out_sems.at[2, b]),
+            pltpu.make_async_copy(inv_ref.at[b], inv_hbm.at[part * blocks + b], out_sems.at[3, b]),
         )
 
     def finish(b, _):
@@ -191,7 +194,12 @@
         for c in range(near):
             tile = acc[b * wide + c]
             total += tile
-            ref, at = (al_ref, c) if c < cols[0] else (bound_ref, c - cols[0])
+            if c < cols[0]:
+                ref, at = al_ref, c
+            elif c < cols[0] + cols[1] // 2:
+                ref, at = kept_ref, c - cols[0]
+            else:
+                ref, at = bound_ref, c - cols[0] - cols[1] // 2
             ref[rows, at * size : (at + 1) * size] = tile.astype(BF16)
         for q in range(cols[2] // 2):
             pair = [acc[b * wide + near + 2 * q + i] for i in range(2)]
@@ -200,7 +208,7 @@
             own_ref[rows, q * size : (q + 1) * size] = moved[:, :size]
             other_ref[rows, q * size : (q + 1) * size] = moved[:, size:]
         deg = 1.0 + jnp.sum(total, axis=1, keepdims=True)
-        inv_ref[rows, :] = jnp.broadcast_to(1.0 / deg, (size, size))
+        inv_ref[b] = jnp.broadcast_to(1.0 / deg, (size, size)).T[0:8, :]
         for copy in leave(b):
             copy.start()
         agg_ref[rows, :] = dot(al_ref[rows, :], x_ref[...])
@@ -227,13 +235,31 @@
 
 
 def stage_kernel(
-    send_rows, parts, lists_hbm, hub_hbm, got_ref, agg_ref, own_ref, bound_in, other_in, sel_ref, sum_ref, *refs
+    send_rows,
+    parts,
+    lists_hbm,
+    hub_hbm,
+    got_ref,
+    inv_hbm,
+    agg_ref,
+    own_ref,
+    kept_ref,
+    bound_in,
+    other_in,
+    sel_ref,
+    sum_ref,
+    inv_ref,
+    *refs,
 ):
-    moved, (lists_ref, hub_ref, x_ref, sems) = refs[:-4], refs[-4:]
+    moved, (lists_ref, hub_ref, inv_row, x_ref, sems) = refs[:-5], refs[-5:]
     part = pl.program_id(0)
     per = got_ref.shape[1]
-    rows, bound = bound_in.shape if parts > 1 else moved[0].shape
-    copies = fetch(((lists_hbm, lists_ref), (hub_hbm, hub_ref), *zip((bound_in, other_in), moved)), sems)
+    rows, half = kept_ref.shape
+    bound = 2 * half
+    blocks, _, size = inv_row.shape
+    inv_part = inv_hbm.at[pl.ds(part * blocks, blocks)]
+    small = ((lists_hbm, lists_ref), (hub_hbm, hub_ref), (inv_part, inv_row))
+    copies = fetch((*small, *zip((bound_in, other_in), moved)), sems)
 
     @pl.when(part == 0)
     def _():
@@ -247,14 +273,19 @@
     def _():
         fill_select(lists_ref, hub_ref, sel_ref)
 
+    copies[2].wait()
+    for b in range(blocks):
+        inv_ref[b * size : (b + 1) * size, :] = jnp.broadcast_to(inv_row[b, 0:1, :], (size, size)).T
+
     if moved:
-        copies[2].wait()
+        copies[3].wait()
     bound_ref = moved[0] if moved else bound_in
     for at in cuts_of(rows, 4):
-        total = dot(own_ref[at, :], x_ref[bound:, :]) + dot(bound_ref[at, :], x_ref[0:bound, :])
+        total = dot(own_ref[at, :], x_ref[bound:, :]) + dot(kept_ref[at, :], x_ref[0:half, :])
+        total += dot(bound_ref[at, :], x_ref[half:bound, :])
         sum_ref[at, :] = agg_ref[at, :] + total
     if moved:
-        copies[3].wait()
+        copies[4].wait()
 
 
 def mean_kernel(send_rows, parts, got_ref, sum_ref, a_ref, inv_ref, sel_ref, mean_ref, send_ref, x_ref):
@@ -289,6 +320,7 @@
     got_one,
     got_two,
     local_ref,
+    kept_ref,
     bound_ref,
     own_ref,
     self_one,
@@ -303,7 +335,8 @@
     part = pl.program_id(0)
     rows = local_ref.shape[0]
     nodes, width = x_ref.shape
-    near = nodes + bound_ref.shape[1]
+    middle = nodes + kept_ref.shape[1]
+    near = middle + bound_ref.shape[1]
 
     @pl.when(part == 0)
     def _():
@@ -317,7 +350,8 @@
     for at in cuts_of(rows, 4):
         sum_ref[at, :] = (
             dot(local_ref[at, :], first[0:nodes, :])
-            + dot(bound_ref[at, :], first[nodes:near, :])
+            + dot(kept_ref[at, :], first[nodes:middle, :])
+            + dot(bound_ref[at, :], first[middle:near, :])
             + dot(own_ref[at, :], first[near:, :])
         )
     at = pl.ds(pl.multiple_of(part * rows, rows), rows)
@@ -441,30 +475,32 @@
     chunks = 2
     bound = peers * send_rows
     other_rows = peers * (hubs // 2)
-    a_local, a_bound, a_other, a_own, inv, agg = pl.pallas_call(
+    a_local, a_bound, a_other, inv, a_kept, a_own, agg = pl.pallas_call(
         functools.partial(build_kernel, cols, hubs, parts, chunks),
         out_shape=(
             pltpu.HBM((nodes, nodes), BF16),
-            pltpu.HBM((nodes, bound), BF16),
+            pltpu.HBM((nodes, bound // 2), BF16),
             pltpu.HBM((nodes, other_rows), BF16),
+            pltpu.HBM((blocks, 8, size), F32),
+            kept((nodes, bound // 2), BF16),
             kept((nodes, other_rows), BF16),
-            kept((nodes, size), F32),
             kept((nodes, f_in), F32),
         ),
         grid=(parts,),
         in_specs=[whole(pltpu.SMEM)] * 6 + [hbm] * 4,
-        out_specs=(hbm, hbm, hbm, split(other_rows), split(size), split(f_in)),
+        out_specs=(hbm, hbm, hbm, hbm, split(bound // 2), split(other_rows), split(f_in)),
         scratch_shapes=[
             pltpu.VMEM((blocks // parts * wide + spare, size, size), F32),
             pltpu.VMEM((3, tiles, size, size), BF16),
             pltpu.VMEM((nodes, f_in), BF16),
             pltpu.VMEM((2 * size, 2 * size), BF16),
             pltpu.VMEM((rows, nodes), BF16),
-            pltpu.VMEM((rows, bound), BF16),
+            pltpu.VMEM((rows, bound // 2), BF16),
             pltpu.VMEM((rows, other_rows), BF16),
+            pltpu.VMEM((blocks // parts, 8, size), F32),
             dma((3, chunks)),
             dma(()),
-            dma((3, blocks // parts)),
+            dma((4, blocks // parts)),
         ],
         compiler_params=params(36 if parts == 1 else 48),
         cost_estimate=pl.CostEstimate(flops=2 * nodes * nodes * f_in, bytes_accessed=40 * MIB, transcendentals=0),
@@ -473,29 +509,35 @@
         *in_hbm(local_dst, local_src, remote_dst, remote_src, hub_dst, hub_src),
         *in_hbm(features, local_tiles, remote_tiles, hub_tiles),
     )
-    built = (got, a_local, a_bound, a_other, a_own, inv, agg)
-    got, a_local, a_bound, a_other, a_own, inv, agg = lax.optimization_barrier(built)
+    built = (got, a_local, a_bound, a_other, inv, a_kept, a_own, agg)
+    got, a_local, a_bound, a_other, inv, a_kept, a_own, agg = lax.optimization_barrier(built)
 
     other = lax.ppermute(got, "nodes", swap)
 
     far = (a_bound, a_other)
     moved = far if parts == 1 else ()
-    sel, agg, *moved = pl.pallas_call(
+    sel, agg, inv, *moved = pl.pallas_call(
         functools.partial(stage_kernel, send_rows, parts),
         out_shape=(
             kept((chosen, nodes), BF16),
             kept((nodes, f_in), F32),
+            kept((nodes, size), F32),
             *(kept(x.shape, x.dtype) for x in moved),
         ),
         grid=(parts,),
-        in_specs=[hbm, hbm, vm, split(f_in), split(other_rows)]
-        + ([hbm, hbm] if moved else [split(bound), whole(pl.ANY)]),
-        out_specs=(vm, split(f_in), *([vm] * len(moved))),
-        scratch_shapes=[*tables, pltpu.VMEM((bound + other_rows, f_in), BF16), dma((2 + len(moved),))],
+        in_specs=[hbm, hbm, vm, hbm, split(f_in), split(other_rows), split(bound // 2)]
+        + ([hbm, hbm] if moved else [split(bound // 2), whole(pl.ANY)]),
+        out_specs=(vm, split(f_in), split(size), *([vm] * len(moved))),
+        scratch_shapes=[
+            *tables,
+            pltpu.VMEM((blocks // parts, 8, size), F32),
+            pltpu.VMEM((bound + other_rows, f_in), BF16),
+            dma((3 + len(moved),)),
+        ],
         compiler_params=params(12 if parts == 1 else 32),
         cost_estimate=pl.CostEstimate(flops=0, bytes_accessed=8 * MIB, transcendentals=0),
         name="stage",
-    )(*in_hbm(lists, hub_row), got, agg, a_own, *(in_hbm(*far) if moved else far))
+    )(*in_hbm(lists, hub_row), got, *in_hbm(inv), agg, a_own, a_kept, *(in_hbm(*far) if moved else far))
     if moved:
         a_bound, a_other = moved
 
@@ -519,7 +561,7 @@
         functools.partial(own_kernel, send_rows),
         out_shape=(sds((nodes, hid), F32), sds((nodes, hid), F32)),
         grid=(parts,),
-        in_specs=[vm] * 4 + [split(nodes), split(bound), split(other_rows)] + [vm] * 3,
+        in_specs=[vm] * 4 + [split(nodes), split(bound // 2), split(bound // 2), split(other_rows)] + [vm] * 3,
         out_specs=(split(hid), split(hid)),
         scratch_shapes=[
             pltpu.VMEM((near, 2 * f_in), BF16),
@@ -529,7 +571,7 @@
         compiler_params=params(16 if parts == 1 else 48),
         cost_estimate=pl.CostEstimate(flops=2 * nodes * near * hid, bytes_accessed=8 * MIB, transcendentals=0),
         name="own",
-    )(features, mean, got, got_two, a_local, a_bound, a_own, self_one, neigh_one, self_two)
+    )(features, mean, got, got_two, a_local, a_kept, a_bound, a_own, self_one, neigh_one, self_two)
 
     return pl.pallas_call(
         functools.partial(last_kernel, send_rows),

time: 46.7 us -> 46.6 us (level)
  no operation moved by 1% of the time
where the time goes in v6:
time: 46.6 us; the launch traced here: 46.2 us
  Pallas kernels  18.7 us (40%)
  blocking collectives  15.7 us (34%)
  starting transfers between devices  7.31 us (16%)
  waiting for transfers between devices  4.22 us (9%)
    all_to_all x1, blocking collectives, per_device(): lax.all_to_all(send, 'nodes', split_axis=0, concat_axis=0, tiled=True)  15.7 us
    pallas_call x1, Pallas kernels, per_device(): pl.pallas_call(functools.partial(build_kernel, cols, hubs, parts, chunks)...  8.95 us
    all_to_all x1, starting transfers between devices, per_device(): got = lax.all_to_all(send, 'nodes', split_axis=0, concat_axis=0, tiled=True)  7.3 us
    all_to_all x1, waiting for transfers between devices, per_device(): got = lax.all_to_all(send, 'nodes', split_axis=0, concat_axis=0, tiled=True)  4.22 us
    pallas_call x1, Pallas kernels, per_device(): pl.pallas_call(functools.partial(own_kernel, send_rows), out_shape=(sds((...  2.3 us
    pallas_call x1, Pallas kernels, per_device(): pl.pallas_call(select_kernel, out_shape=kept((peers, per, f_in), BF16), i...  2.25 us
    pallas_call x1, Pallas kernels, per_device(): pl.pallas_call(functools.partial(stage_kernel, send_rows, parts), out_sha...  2.18 us
    pallas_call x1, Pallas kernels, per_device(): pl.pallas_call(functools.partial(last_kernel, send_rows), out_shape=sds((...  1.99 us
  transfers between devices with their start and end apart: 3, of which 1 were waited for; matrix products, arithmetic and copies ran while one was open for 0% of the time, Pallas kernels for 29%

profile of v6, /device:TPU:0, one launch (start us, length us, event | category | flops | bytes accessed | tf_op | source)
XLA Modules:
  0.0 46.2 jit_solution(11198794494384517512)
XLA Ops:
  0.0 2.3 %select.1 = bf16[32,48,128]{2,1,0:T(8,128)(2,1)} custom-call(bf16[1024,128]{1,0:T(8,128)(2,1)} %x_ref.1, s32[16,32]{1,0:T(8,128)} %bitcast.4, s32[1,64]{1,0:T(1,128)} %bitcast.6), custom_call_target="tpu_custom_call" | custom-call | tf_op jit(solution)/shard_map/select/pallas_call | solution.py:463
  2.3 7.3 %all-to-all-start = ((bf16[32,48,128]{2,1,0:T(8,128)(2,1)}), bf16[32,48,128]{2,1,0:T(8,128)(2,1)S(1)}, u32[]{:S(2)}, u32[]{:S(2)}) async-start(bf16[32,48,128]{2,1,0:T(8,128)(2,1)} %select.1), calls=%async_computation | async-start | bytes 786432 | tf_op jit(solution)/shard_map/all_to_all | solution.py:473
  9.6 9.0 %build.1 = (bf16[1024,1024]{1,0:T(8,128)(2,1)}, bf16[1024,256]{1,0:T(8,128)(2,1)}, bf16[1024,1024]{1,0:T(8,128)(2,1)}, f32[8,8,128]{2,1,0:T(8,128)}, bf16[1024,2...) custom-call(s32[96]{0:T(128)} %ld.1, s32[96]{0:T(128)} %ls.1, s32[96]{0:T(128)} %rd.1, ...), custom_call_target="tpu_custom_call" | custom-call | flops 268435456 | bytes 41943040 | tf_op jit(solution)/shard_map/build/pallas_call | solution.py:478
  18.5 4.2 %all-to-all-done.got_ref.got_one = bf16[32,48,128]{2,1,0:T(8,128)(2,1)S(1)} async-done(((bf16[32,48,128]{2,1,0:T(8,128)(2,1)}), bf16[32,48,128]{2,1,0:T(8,128)(2,1)S(1)}, u32[]{:S(2)}, u32[]{:S(2)}) %all-to-all-start) | async-done | bytes 393248 | tf_op jit(solution)/shard_map/all_to_all | solution.py:473
  22.7 0.0 collective-permute-start
  22.8 2.2 %stage.1 = (bf16[576,1024]{1,0:T(8,128)(2,1)S(1)}, f32[1024,128]{1,0:T(8,128)S(1)}, f32[1024,128]{1,0:T(8,128)S(1)}, bf16[1024,256]{1,0:T(8,128)(2,1)S(1)}, bf16[1024,1024]{1,0:T(8,128)(2,1)S(1)}) custom-call(s32[16,32]{1,0:T(8,128)} %bitcast.5, s32[1,64]{1,0:T(1,128)} %bitcast.7, bf16[32,48,128]{2,1,0:T(8,128)(2,1)S(1)} %all-to-all-done.got_ref.got_one, ...), custom_call_target="tpu_custom_call" | custom-call | bytes 8388608 | tf_op jit(solution)/shard_map/stage/pallas_call | solution.py:519
  24.9 0.0 collective-permute-done.got_ref.got_one
  25.0 0.0 copy-start
  25.0 0.0 copy-start.1
  25.0 0.0 copy-start.2
  25.0 0.0 copy-start.3
  25.0 0.0 copy-start.4
  25.0 1.1 %mean.1 = (bf16[1024,128]{1,0:T(8,128)(2,1)S(1)}, bf16[32,48,128]{2,1,0:T(8,128)(2,1)S(1)}) custom-call(bf16[32,48,128]{2,1,0:T(8,128)(2,1)S(1)} %collective-permute-done.got_ref.got_one, f32[1024,128]{1,0:T(8,128)S(1)} %get-tuple-element.45.sum_ref, bf16[1024,1024]{1,0:T(8,128)(2,1)S(1)} %get-tuple-element.46.a_ref, ...), custom_call_target="tpu_custom_call" | custom-call | tf_op jit(solution)/shard_map/mean/pallas_call | solution.py:544
  26.1 15.7 %all_to_all.10.got_two = bf16[32,48,128]{2,1,0:T(8,128)(2,1)S(1)} all-to-all(bf16[32,48,128]{2,1,0:T(8,128)(2,1)S(1)} %get-tuple-element.49), channel_id=1, replica_groups=mesh['nodes'=32] {'nodes'}, dimensions={0} | all-to-all | bytes 786432 | tf_op jit(solution)/shard_map/all_to_all | solution.py:555
  41.8 0.0 collective-permute-start.1
  41.8 0.0 copy-done
  41.8 0.0 copy-done.1
  41.8 0.0 copy-done.2
  41.8 0.0 copy-done.3
  41.8 0.0 copy-done.4
  41.9 0.0 copy-start.5
  41.9 2.3 %own.1 = (f32[1024,256]{1,0:T(8,128)S(1)}, f32[1024,256]{1,0:T(8,128)S(1)}) custom-call(bf16[1024,128]{1,0:T(8,128)(2,1)S(1)} %copy-done, bf16[1024,128]{1,0:T(8,128)(2,1)S(1)} %get-tuple-element.52.mean_ref, bf16[32,48,128]{2,1,0:T(8,128)(2,1)S(1)} %all-to-all-done.got_ref.got_one, bf16[32,48,128]{2,1,0:T(8,128)(2,1)S(1)} %all_to_all.10.got_two, ...), custom_call_target="tpu_custom_call" | custom-call | flops 1342177280 | bytes 8388608 | tf_op jit(solution)/shard_map/own/pallas_call | solution.py:560
  44.2 0.0 collective-permute-done.1.got_two
  44.2 0.0 copy-done.5
  44.2 2.0 %last.1 = f32[1024,256]{1,0:T(8,128)} custom-call(bf16[32,48,128]{2,1,0:T(8,128)(2,1)S(1)} %collective-permute-done.got_ref.got_one, bf16[32,48,128]{2,1,0:T(8,128)(2,1)S(1)} %collective-permute-done.1.got_two, f32[1024,256]{1,0:T(8,128)S(1)} %get-tuple-element.55.sum_ref, f32[1024,256]{1,0:T(8,128)S(1)} %get-tuple-element.56.part_ref, ...), custom_call_target="tpu_custom_call" | custom-call | tf_op jit(solution)/shard_map/last/pallas_call | solution.py:576
Async XLA Ops:
  2.3 20.5 %all-to-all-start = ((bf16[32,48,128]{2,1,0:T(8,128)(2,1)}), bf16[32,48,128]{2,1,0:T(8,128)(2,1)S(1)}, u32[]{:S(2)}, u32[]{:S(2)}) async-start(bf16[32,48,128]{2,1,0:T(8,128)(2,1)} %select.1), calls=%async_computation | async-start | bytes 786432 | tf_op jit(solution)/shard_map/all_to_all | solution.py:473
  22.7 2.2 %collective-permute-start = (bf16[32,48,128]{2,1,0:T(8,128)(2,1)S(1)}, bf16[32,48,128]{2,1,0:T(8,128)(2,1)S(1)}, u32[]{:S(2)}, u32[]{:S(2)}) collective-permute-start(bf16[32,48,128]{2,1,0:T(8,128)(2,1)S(1)} %all-to-all-done.got_ref.got_one), channel_id=1, source_target_pairs={{0,1},{1,0},{2,3},{3,2},{4,5},{5,4},{6,7},{7,6},{8,9},{9,8},{10,11... | collective-permute-start | bytes 1179656 | tf_op jit(solution)/shard_map/ppermute | solution.py:515
  25.0 16.9 %copy-start = (bf16[1024,128]{1,0:T(8,128)(2,1)S(1)}, bf16[1024,128]{1,0:T(8,128)(2,1)}, u32[]{:S(2)}) copy-start(bf16[1024,128]{1,0:T(8,128)(2,1)} %x_ref.1) | copy-start | bytes 786436
  25.0 16.9 %copy-start.1 = (bf16[1024,1024]{1,0:T(8,128)(2,1)S(1)}, bf16[1024,1024]{1,0:T(8,128)(2,1)}, u32[]{:S(2)}) copy-start(bf16[1024,1024]{1,0:T(8,128)(2,1)} %get-tuple-element.53.local_ref) | copy-start | bytes 6291460
  25.0 16.8 %copy-start.2 = (bf16[128,256]{1,0:T(8,128)(2,1)S(1)}, bf16[128,256]{1,0:T(8,128)(2,1)}, u32[]{:S(2)}) copy-start(bf16[128,256]{1,0:T(8,128)(2,1)} %self_one.3) | copy-start | bytes 196612
  25.0 16.8 %copy-start.3 = (bf16[128,256]{1,0:T(8,128)(2,1)S(1)}, bf16[128,256]{1,0:T(8,128)(2,1)}, u32[]{:S(2)}) copy-start(bf16[128,256]{1,0:T(8,128)(2,1)} %neigh_one.3) | copy-start | bytes 196612
  25.0 16.8 %copy-start.4 = (bf16[256,256]{1,0:T(8,128)(2,1)S(1)}, bf16[256,256]{1,0:T(8,128)(2,1)}, u32[]{:S(2)}) copy-start(bf16[256,256]{1,0:T(8,128)(2,1)} %self_two.1) | copy-start | bytes 393220
  41.8 2.4 %collective-permute-start.1 = (bf16[32,48,128]{2,1,0:T(8,128)(2,1)S(1)}, bf16[32,48,128]{2,1,0:T(8,128)(2,1)S(1)}, u32[]{:S(2)}, u32[]{:S(2)}) collective-permute-start(bf16[32,48,128]{2,1,0:T(8,128)(2,1)S(1)} %all_to_all.10.got_two), channel_id=1, source_target_pairs={{0,1},{1,0},{2,3},{3,2},{4,5},{5,4},{6,7},{7,6},{8,9},{9,8},{10,11... | collective-permute-start | bytes 1179656 | tf_op jit(solution)/shard_map/ppermute | solution.py:557
  41.9 2.3 %copy-start.5 = (bf16[256,256]{1,0:T(8,128)(2,1)S(1)}, bf16[256,256]{1,0:T(8,128)(2,1)}, u32[]{:S(2)}) copy-start(bf16[256,256]{1,0:T(8,128)(2,1)} %neigh_two.1) | copy-start | bytes 393220
